TPU v7x, 32 devices: a whole 2x2x4 slice. The times are simulated.
32 devices in a mesh: row: 4 (over y, x), col: 8 (over z, core).
Axes of the slice: x: 2, y: 2, z: 4, core: 2. Of those that a mesh axis runs over, the one named last changes fastest.
Arguments:
- spectra: bfloat16 [1024, 8, 1536], P(('row', 'col')), may hold values from -6 to 6
- pair_bins: int32 [4, 1024, 32], P(None, ('row', 'col')), may hold values from 0 to 127
- dead_mask: int32 [1024], P(('row', 'col')), may hold values 0 or 1
Outputs:
- stacked_lags: float32 [128, 896], P(('row', 'col'))
All inputs are finite; a program needn't handle non-finite values. No bound on the sum of `dead_mask` on one device may be relied on, other than what follows from the above.
Results may differ from a plain program's by a relative error of at most 0.0041.
Values may be sent and summed in bfloat16 or wider, within the bound.
No kernel may reach another device: no remote copies, remote signals or barrier semaphores. Data moves between devices by JAX's collectives and lax.ppermute only.
A program may use at most 256 MiB of HBM per device.

v0:
```python
import math

import jax
import jax.numpy as jnp
from jax import lax
from jax.sharding import PartitionSpec as P

NT = 1600
LAGS = 896
NB = 128
ROUNDS = 4


def swapped(value, axis, stride):
    mask = 2**stride
    pairs = [(source, source ^ mask) for source in range(lax.axis_size(axis))]
    return lax.ppermute(value, axis, pairs)


def whiten(spectra, dead_mask):
    values = spectra.astype(jnp.float32)
    powers = jnp.mean(values * values, axis=-1, keepdims=True)
    alive = dead_mask.astype(jnp.float32)[:, None, None]
    return (values / jnp.sqrt(powers + 1e-06) * alive).astype(jnp.bfloat16)


def cross_spectra(local_part, remote_part):
    half_len = local_part.shape[-1] // 2
    one_real, one_imag = (local_part[..., :half_len], local_part[..., half_len:])
    two_real, two_imag = (remote_part[..., :half_len], remote_part[..., half_len:])
    real_part = jnp.einsum(
        "iwk,jwk->ijk", one_real, two_real, preferred_element_type=jnp.float32
    ) + jnp.einsum("iwk,jwk->ijk", one_imag, two_imag, preferred_element_type=jnp.float32)
    imag_part = jnp.einsum(
        "iwk,jwk->ijk", one_imag, two_real, preferred_element_type=jnp.float32
    ) - jnp.einsum("iwk,jwk->ijk", one_real, two_imag, preferred_element_type=jnp.float32)
    channels = local_part.shape[0]
    return jnp.concatenate([real_part, imag_part], axis=-1).reshape(
        channels * remote_part.shape[0], 2 * half_len
    )


def build_table(freq_len, lag_len, length):
    freq_ids = jnp.arange(freq_len, dtype=jnp.int32)
    lag_ids = jnp.arange(lag_len, dtype=jnp.int32) - lag_len // 2
    phases = freq_ids[:, None] * lag_ids[None, :] % length
    angles = phases.astype(jnp.float32) * (2.0 * math.pi / length)
    weights = jnp.where(freq_ids == 0, 1.0, 2.0).astype(jnp.float32)[:, None]
    return jnp.concatenate([weights * jnp.cos(angles), -weights * jnp.sin(angles)], axis=0)


def one_hot_bins(bin_ids):
    bin_range = jnp.arange(NB, dtype=jnp.int32)
    return (bin_ids.reshape(-1)[:, None] == bin_range[None, :]).astype(jnp.float32)


def stack_bins(hot_rows, values):
    return lax.dot_general(
        hot_rows, values, (((0,), (0,)), ((), ())), precision=lax.Precision.HIGHEST
    )


def on_device(spectra, pair_bins, dead_mask):
    whitened = whiten(spectra, dead_mask)
    block_size = spectra.shape[0]
    width = spectra.shape[1]
    freq_len = spectra.shape[2] // 2
    groups = lax.axis_size("row") * lax.axis_size("col")
    stacked = jnp.zeros((NB, 2 * freq_len), jnp.float32)
    for round_no in range(ROUNDS):
        remote_part = swapped(whitened, ("row", "col"), round_no)
        stacked = stacked + stack_bins(
            one_hot_bins(pair_bins[round_no]), cross_spectra(whitened, remote_part)
        )
    pairs = ROUNDS * block_size * block_size * groups // NB
    scaling = 1.0 / (2.0 * math.sqrt(freq_len * width * pairs))
    table = build_table(freq_len, LAGS, NT)
    owned = lax.psum_scatter(stacked, ("row", "col"), scatter_dimension=0, tiled=True)
    result = jnp.dot(owned, table, precision=lax.Precision.HIGHEST) * scaling
    return result


def solution(mesh):
    return jax.shard_map(
        on_device,
        mesh=mesh,
        in_specs=(P(("row", "col"), None, None), P(None, ("row", "col"), None), P(("row", "col"))),
        out_specs=P(("row", "col"), None),
        check_vma=False,
    )
```

profile of v0, /device:TPU:1, one launch (start us, length us, event | category | flops | bytes accessed | tf_op | source)
XLA Modules:
  0.0 442.1 jit_solution(1987324940695362109)
XLA Ops:
  29.1 6.8 %fusion.31 = f32[768,32,32]{2,1,0:T(8,128)} fusion(bf16[32,8,768]{0,1,2:T(8,128)(2,1)} %copy.64, bf16[32,8,768]{0,1,2:T(8,128)(2,1)S(1)} %copy.34), kind=kOutput, calls=%fused_computation.57 | convolution fusion | flops 12582912 | bytes 3932160 | tf_op jit(solution)/shard_map/iwk,jwk->ijk/dot_general | solution.py:33
  35.9 5.5 %fusion.32 = f32[768,32,32]{2,1,0:T(8,128)} fusion(bf16[32,8,768]{0,1,2:T(8,128)(2,1)S(1)} %copy-done.1, bf16[32,8,768]{0,1,2:T(8,128)(2,1)S(1)} %copy.32), kind=kOutput, calls=%fused_computation.58 | convolution fusion | flops 12582912 | bytes 3932160 | tf_op jit(solution)/shard_map/iwk,jwk->ijk/dot_general | solution.py:36
  41.4 7.2 %collective-permute-done.1 = bf16[32,8,1536]{2,1,0:T(8,128)(2,1)} collective-permute-done((bf16[32,8,1536]{2,1,0:T(8,128)(2,1)}, bf16[32,8,1536]{2,1,0:T(8,128)(2,1)}, u32[]{:S(2)}, u32[]{:S(2)}) %collective-permute-start.1) | collective-permute-done | bytes 786464 | tf_op jit(solution)/shard_map/ppermute | solution.py:17
  50.7 3.0 copy.66
  53.7 6.8 %fusion.33 = f32[768,32,32]{2,1,0:T(8,128)} fusion(bf16[32,8,768]{0,1,2:T(8,128)(2,1)} %copy.66, bf16[32,8,768]{0,1,2:T(8,128)(2,1)S(1)} %copy.34), kind=kOutput, calls=%fused_computation.59 | convolution fusion | flops 12582912 | bytes 3932160 | tf_op jit(solution)/shard_map/iwk,jwk->ijk/dot_general | solution.py:33
  60.4 5.5 %fusion.34 = f32[768,32,32]{2,1,0:T(8,128)} fusion(bf16[32,8,768]{0,1,2:T(8,128)(2,1)S(1)} %copy-done.2, bf16[32,8,768]{0,1,2:T(8,128)(2,1)S(1)} %copy.32), kind=kOutput, calls=%fused_computation.60 | convolution fusion | flops 12582912 | bytes 3932160 | tf_op jit(solution)/shard_map/iwk,jwk->ijk/dot_general | solution.py:36
  68.0 3.0 copy.68
  71.0 6.8 %fusion.35 = f32[768,32,32]{2,1,0:T(8,128)} fusion(bf16[32,8,768]{0,1,2:T(8,128)(2,1)} %copy.68, bf16[32,8,768]{0,1,2:T(8,128)(2,1)S(1)} %copy.34), kind=kOutput, calls=%fused_computation.61 | convolution fusion | flops 12582912 | bytes 3932160 | tf_op jit(solution)/shard_map/iwk,jwk->ijk/dot_general | solution.py:33
  77.8 5.5 %fusion.36 = f32[768,32,32]{2,1,0:T(8,128)} fusion(bf16[32,8,768]{0,1,2:T(8,128)(2,1)S(1)} %copy-done.3, bf16[32,8,768]{0,1,2:T(8,128)(2,1)S(1)} %copy.32), kind=kOutput, calls=%fused_computation.62 | convolution fusion | flops 12582912 | bytes 3932160 | tf_op jit(solution)/shard_map/iwk,jwk->ijk/dot_general | solution.py:36
  88.4 6.9 %fusion.37 = f32[768,32,32]{2,1,0:T(8,128)} fusion(bf16[32,8,768]{0,1,2:T(8,128)(2,1)} %copy.70, bf16[32,8,768]{0,1,2:T(8,128)(2,1)S(1)} %copy.34), kind=kOutput, calls=%fused_computation.63 | convolution fusion | flops 12582912 | bytes 3932160 | tf_op jit(solution)/shard_map/iwk,jwk->ijk/dot_general | solution.py:33
  95.3 5.4 %fusion.38 = f32[768,32,32]{2,1,0:T(8,128)} fusion(bf16[32,8,768]{0,1,2:T(8,128)(2,1)S(1)} %copy-done.4, bf16[32,8,768]{0,1,2:T(8,128)(2,1)S(1)} %copy.32), kind=kOutput, calls=%fused_computation.64 | convolution fusion | flops 12582912 | bytes 3932160 | tf_op jit(solution)/shard_map/iwk,jwk->ijk/dot_general | solution.py:36
  102.6 8.8 %add_bitcast_fusion.3 = f32[32,32,768]{0,1,2:T(8,128)} fusion(f32[768,32,32]{2,1,0:T(8,128)} %fusion.31, bf16[32,8,768]{0,1,2:T(8,128)(2,1)} %copy.63, bf16[32,8,768]{0,1,2:T(8,128)(2,1)S(1)} %copy.32), kind=kOutput, calls=%fused_computation.7 | convolution fusion | flops 13369344 | bytes 7077888 | tf_op jit(solution)/shard_map/iwk,jwk->ijk/dot_general | solution.py:31
  111.4 11.2 %copy.37 = f32[32,32,768]{2,1,0:T(8,128)} copy(f32[32,32,768]{0,1,2:T(8,128)} %add_bitcast_fusion.3) | data formatting | bytes 6291456 | tf_op jit(solution)/shard_map/add | solution.py:31
  122.6 8.7 %subtract_bitcast_fusion.3 = f32[32,32,768]{0,1,2:T(8,128)} fusion(f32[768,32,32]{2,1,0:T(8,128)} %fusion.32, bf16[32,8,768]{0,1,2:T(8,128)(2,1)} %copy.63, bf16[32,8,768]{0,1,2:T(8,128)(2,1)S(1)} %copy.34), kind=kOutput, calls=%fused_computation.6 | convolution fusion | flops 13369344 | bytes 7077888 | tf_op jit(solution)/shard_map/iwk,jwk->ijk/dot_general | solution.py:34
  131.4 11.1 %copy.38 = f32[32,32,768]{2,1,0:T(8,128)} copy(f32[32,32,768]{0,1,2:T(8,128)} %subtract_bitcast_fusion.3) | data formatting | bytes 6291456 | tf_op jit(solution)/shard_map/sub | solution.py:34
  144.4 8.7 %add_bitcast_fusion.2 = f32[32,32,768]{0,1,2:T(8,128)} fusion(f32[768,32,32]{2,1,0:T(8,128)} %fusion.33, bf16[32,8,768]{0,1,2:T(8,128)(2,1)} %copy.65, bf16[32,8,768]{0,1,2:T(8,128)(2,1)S(1)} %copy.32), kind=kOutput, calls=%fused_computation.5 | convolution fusion | flops 13369344 | bytes 7077888 | tf_op jit(solution)/shard_map/iwk,jwk->ijk/dot_general | solution.py:31
  153.1 11.0 %copy.45 = f32[32,32,768]{2,1,0:T(8,128)} copy(f32[32,32,768]{0,1,2:T(8,128)} %add_bitcast_fusion.2) | data formatting | bytes 6291456 | tf_op jit(solution)/shard_map/add | solution.py:31
  164.1 8.7 %subtract_bitcast_fusion.2 = f32[32,32,768]{0,1,2:T(8,128)} fusion(f32[768,32,32]{2,1,0:T(8,128)} %fusion.34, bf16[32,8,768]{0,1,2:T(8,128)(2,1)} %copy.65, bf16[32,8,768]{0,1,2:T(8,128)(2,1)S(1)} %copy.34), kind=kOutput, calls=%fused_computation.4 | convolution fusion | flops 13369344 | bytes 7077888 | tf_op jit(solution)/shard_map/iwk,jwk->ijk/dot_general | solution.py:34
  172.8 11.1 %copy.46 = f32[32,32,768]{2,1,0:T(8,128)} copy(f32[32,32,768]{0,1,2:T(8,128)} %subtract_bitcast_fusion.2) | data formatting | bytes 6291456 | tf_op jit(solution)/shard_map/sub | solution.py:34
  185.8 8.7 %add_bitcast_fusion.1 = f32[32,32,768]{0,1,2:T(8,128)} fusion(f32[768,32,32]{2,1,0:T(8,128)} %fusion.35, bf16[32,8,768]{0,1,2:T(8,128)(2,1)} %copy.67, bf16[32,8,768]{0,1,2:T(8,128)(2,1)S(1)} %copy.32), kind=kOutput, calls=%fused_computation.3 | convolution fusion | flops 13369344 | bytes 7077888 | tf_op jit(solution)/shard_map/iwk,jwk->ijk/dot_general | solution.py:31
  194.5 11.0 %copy.53 = f32[32,32,768]{2,1,0:T(8,128)} copy(f32[32,32,768]{0,1,2:T(8,128)} %add_bitcast_fusion.1) | data formatting | bytes 6291456 | tf_op jit(solution)/shard_map/add | solution.py:31
  205.5 8.7 %subtract_bitcast_fusion.1 = f32[32,32,768]{0,1,2:T(8,128)} fusion(f32[768,32,32]{2,1,0:T(8,128)} %fusion.36, bf16[32,8,768]{0,1,2:T(8,128)(2,1)} %copy.67, bf16[32,8,768]{0,1,2:T(8,128)(2,1)S(1)} %copy.34), kind=kOutput, calls=%fused_computation.2 | convolution fusion | flops 13369344 | bytes 7077888 | tf_op jit(solution)/shard_map/iwk,jwk->ijk/dot_general | solution.py:34
  214.2 23.0 %copy.54 = f32[32,32,768]{2,1,0:T(8,128)} copy(f32[32,32,768]{0,1,2:T(8,128)} %subtract_bitcast_fusion.1) | data formatting | bytes 6291456 | tf_op jit(solution)/shard_map/sub | solution.py:34
  239.1 8.8 %add_bitcast_fusion = f32[32,32,768]{0,1,2:T(8,128)} fusion(f32[768,32,32]{2,1,0:T(8,128)} %fusion.37, bf16[32,8,768]{0,1,2:T(8,128)(2,1)} %copy.69, bf16[32,8,768]{0,1,2:T(8,128)(2,1)S(1)} %copy.32), kind=kOutput, calls=%fused_computation.1 | convolution fusion | flops 13369344 | bytes 7077888 | tf_op jit(solution)/shard_map/iwk,jwk->ijk/dot_general | solution.py:31
  248.0 11.2 %copy.61 = f32[32,32,768]{2,1,0:T(8,128)} copy(f32[32,32,768]{0,1,2:T(8,128)} %add_bitcast_fusion) | data formatting | bytes 6291456 | tf_op jit(solution)/shard_map/add | solution.py:31
  259.1 8.3 %subtract_bitcast_fusion = f32[32,32,768]{0,1,2:T(8,128)} fusion(f32[768,32,32]{2,1,0:T(8,128)} %fusion.38, bf16[32,8,768]{0,1,2:T(8,128)(2,1)S(1)} %copy-done, bf16[32,8,768]{0,1,2:T(8,128)(2,1)S(1)} %copy.34), kind=kOutput, calls=%fused_computation | convolution fusion | flops 13369344 | bytes 7077888 | tf_op jit(solution)/shard_map/iwk,jwk->ijk/dot_general | solution.py:34
  267.5 11.0 %copy.62 = f32[32,32,768]{2,1,0:T(8,128)} copy(f32[32,32,768]{0,1,2:T(8,128)} %subtract_bitcast_fusion) | data formatting | bytes 6291456 | tf_op jit(solution)/shard_map/sub | solution.py:34
  278.5 3.6 pad_maximum_fusion
  297.3 3.4 convolution_add_fusion
  300.7 12.6 %cosine_multiply_fusion = (f32[768,896]{1,0:T(8,128)}, f32[768,896]{1,0:T(8,128)}) fusion(s32[896]{0:T(1024)S(1)} %iota_add_fusion, f32[768]{0:T(1024)S(1)} %copy-done.16, f32[768]{0:T(1024)S(1)} %copy-done.17), kind=kLoop, calls=%fused_computation.20 | loop fusion | flops 7569408 | bytes 5514752 | tf_op jit(solution)/shard_map/mul | solution.py:49
  313.3 115.9 %all-reduce.3.cloned.1.call-done = f32[128,1536]{1,0:T(8,128)} async-done(((f32[128,1536]{1,0:T(8,128)}), f32[128,1536]{1,0:T(8,128)}) %all-reduce.3.cloned.1.call-update) | async-done | bytes 786448
  429.2 5.8 %fusion.12 = f32[4,896]{1,0:T(4,128)} fusion(f32[768,896]{1,0:T(8,128)} %get-tuple-element.20, f32[768,896]{1,0:T(8,128)} %get-tuple-element.19, f32[128,1536]{1,0:T(8,128)} %all-reduce.3.cloned.1.call-done, u32[]{:T(128)S(6)} %multiply.7), kind=kOutput, calls=%fused_computation.33 | convolution fusion | flops 67440128 | bytes 5543940 | tf_op jit(solution)/shard_map/dot_general | solution.py:79
  (75 shorter events, 54.6 us)
Async XLA Ops:
  6.5 422.7 %all-reduce.3.cloned.1.call-start = ((), (), s32[]{:S(2)}) async-start(), calls=%async_computation | async-start | bytes 1572864
  10.9 13.3 %collective-permute-start = (bf16[32,8,1536]{2,1,0:T(8,128)(2,1)}, bf16[32,8,1536]{2,1,0:T(8,128)(2,1)}, u32[]{:S(2)}, u32[]{:S(2)}) collective-permute-start(bf16[32,8,1536]{2,1,0:T(8,128)(2,1)} %fusion.11), channel_id=1, source_target_pairs={{0,1},{1,0},{2,3},{3,2},{4,5},{5,4},{6,7},{7,6},{8,9},{9,8},{10,11... | collective-permute-start | bytes 2359304 | tf_op jit(solution)/shard_map/ppermute | solution.py:17
  10.9 37.7 %collective-permute-start.1 = (bf16[32,8,1536]{2,1,0:T(8,128)(2,1)}, bf16[32,8,1536]{2,1,0:T(8,128)(2,1)}, u32[]{:S(2)}, u32[]{:S(2)}) collective-permute-start(bf16[32,8,1536]{2,1,0:T(8,128)(2,1)} %fusion.11), channel_id=1, source_target_pairs={{0,2},{1,3},{2,0},{3,1},{4,6},{5,7},{6,4},{7,5},{8,10},{9,11},{10,... | collective-permute-start | bytes 2359304 | tf_op jit(solution)/shard_map/ppermute | solution.py:17
  13.7 52.3 %collective-permute-start.2 = (bf16[32,8,1536]{2,1,0:T(8,128)(2,1)}, bf16[32,8,1536]{2,1,0:T(8,128)(2,1)}, u32[]{:S(2)}, u32[]{:S(2)}) collective-permute-start(bf16[32,8,1536]{2,1,0:T(8,128)(2,1)} %fusion.11), channel_id=1, source_target_pairs={{0,4},{1,5},{2,6},{3,7},{4,0},{5,1},{6,2},{7,3},{8,12},{9,13},{10,... | collective-permute-start | bytes 2359304 | tf_op jit(solution)/shard_map/ppermute | solution.py:17
  16.0 67.3 %collective-permute-start.3 = (bf16[32,8,1536]{2,1,0:T(8,128)(2,1)}, bf16[32,8,1536]{2,1,0:T(8,128)(2,1)}, u32[]{:S(2)}, u32[]{:S(2)}) collective-permute-start(bf16[32,8,1536]{2,1,0:T(8,128)(2,1)} %fusion.11), channel_id=1, source_target_pairs={{0,8},{1,9},{2,10},{3,11},{4,12},{5,13},{6,14},{7,15},{8,0},{9,1},... | collective-permute-start | bytes 2359304 | tf_op jit(solution)/shard_map/ppermute | solution.py:17
  29.1 6.9 %copy-start.1 = (bf16[32,8,768]{0,1,2:T(8,128)(2,1)S(1)}, bf16[32,8,768]{0,1,2:T(8,128)(2,1)}, u32[]{:S(2)}) copy-start(bf16[32,8,768]{0,1,2:T(8,128)(2,1)} %copy.64) | copy-start | bytes 1179652
  53.7 6.8 %copy-start.2 = (bf16[32,8,768]{0,1,2:T(8,128)(2,1)S(1)}, bf16[32,8,768]{0,1,2:T(8,128)(2,1)}, u32[]{:S(2)}) copy-start(bf16[32,8,768]{0,1,2:T(8,128)(2,1)} %copy.66) | copy-start | bytes 1179652
  71.0 6.8 %copy-start.3 = (bf16[32,8,768]{0,1,2:T(8,128)(2,1)S(1)}, bf16[32,8,768]{0,1,2:T(8,128)(2,1)}, u32[]{:S(2)}) copy-start(bf16[32,8,768]{0,1,2:T(8,128)(2,1)} %copy.68) | copy-start | bytes 1179652
  88.4 6.9 %copy-start.4 = (bf16[32,8,768]{0,1,2:T(8,128)(2,1)S(1)}, bf16[32,8,768]{0,1,2:T(8,128)(2,1)}, u32[]{:S(2)}) copy-start(bf16[32,8,768]{0,1,2:T(8,128)(2,1)} %copy.70) | copy-start | bytes 1179652
  131.4 11.1 %copy-start.10 = (bf16[32,8,768]{2,1,0:T(8,128)(2,1)S(1)}, bf16[32,8,768]{2,1,0:T(8,128)(2,1)}, u32[]{:S(2)}) copy-start(bf16[32,8,768]{2,1,0:T(8,128)(2,1)} %get-tuple-element.9) | copy-start | bytes 1179652
  172.8 11.1 %copy-start.11 = (bf16[32,8,768]{2,1,0:T(8,128)(2,1)S(1)}, bf16[32,8,768]{2,1,0:T(8,128)(2,1)}, u32[]{:S(2)}) copy-start(bf16[32,8,768]{2,1,0:T(8,128)(2,1)} %get-tuple-element.7) | copy-start | bytes 1179652
  214.2 23.0 %copy-start.12 = (bf16[32,8,768]{2,1,0:T(8,128)(2,1)S(1)}, bf16[32,8,768]{2,1,0:T(8,128)(2,1)}, u32[]{:S(2)}) copy-start(bf16[32,8,768]{2,1,0:T(8,128)(2,1)} %get-tuple-element.5) | copy-start | bytes 1179652
  248.0 11.2 %copy-start = (bf16[32,8,768]{0,1,2:T(8,128)(2,1)S(1)}, bf16[32,8,768]{0,1,2:T(8,128)(2,1)}, u32[]{:S(2)}) copy-start(bf16[32,8,768]{0,1,2:T(8,128)(2,1)} %copy.69) | copy-start | bytes 1179652
  282.1 2.5 copy-start.5
  282.1 2.8 copy-start.6
  284.9 1.9 copy-start.7
  284.9 2.8 copy-start.8
  287.8 1.9 copy-start.9
  289.7 2.6 copy-start.15
  292.3 2.5 copy-start.14
  294.8 2.5 copy-start.13
  297.3 3.4 copy-start.16
  297.3 3.4 copy-start.17
Sparse Core Ops, SparseCore 0:
  300.8 128.3 all-reduce.2
where the time goes:
time: 448 us; the launch traced here: 442 us
  local copies, waits for them, and re-layouts  138 us (31%)
  matrix products  135 us (30%)
  waiting for transfers between devices  123 us (27%)
  other arithmetic  25.3 us (6%)
  between operations  13.8 us (3%)
  starting transfers between devices  6.32 us (1%)
    unnamed x2, waiting for transfers between devices  116 us
    sub x4, local copies, waits for them, and re-layouts, cross_spectra(): jnp.einsum('iwk,jwk->ijk', one_imag, two_real, preferred_element_type=jnp...  56.1 us
    add x4, local copies, waits for them, and re-layouts, cross_spectra(): jnp.einsum('iwk,jwk->ijk', one_real, two_real, preferred_element_type=jnp...  44.5 us
    dot_general x4, matrix products, cross_spectra(): jnp.einsum('iwk,jwk->ijk', one_real, two_real, preferred_element_type=jnp...  35 us
    dot_general x4, matrix products, cross_spectra(): jnp.einsum('iwk,jwk->ijk', one_imag, two_real, preferred_element_type=jnp...  34.4 us
    dot_general x4, matrix products, cross_spectra(): jnp.einsum('iwk,jwk->ijk', one_imag, two_imag, preferred_element_type=jnp...  27.3 us
    unnamed x44, local copies, waits for them, and re-layouts  23.3 us
    dot_general x4, matrix products, cross_spectra(): jnp.einsum('iwk,jwk->ijk', one_real, two_imag, preferred_element_type=jnp...  21.9 us
  transfers between devices with their start and end apart: 5, of which 2 were waited for; matrix products, arithmetic and copies ran while one was open for 16% of the time, Pallas kernels for 0%

commit v1 on v0

v1 whole, which is shorter than its diff:
```python
import functools
import math

import jax
import jax.numpy as jnp
import numpy as np
from jax import lax
from jax.experimental import pallas as pl
from jax.experimental.pallas import tpu as pltpu
from jax.sharding import PartitionSpec as P

NT = 1600
LAGS = 896
NB = 128
ROUNDS = 4
LANES = 128
AXES = ("row", "col")
F32 = jnp.float32
BF16 = jnp.bfloat16
VMEM_LIMIT = 48 * 2**20


def parity_of(index):
    total = 0
    for bit in range(ROUNDS):
        total = total + ((index >> bit) & 1)
    return total % 2


def swapped(value, stride, groups):
    mask = 2**stride
    return lax.ppermute(value, AXES, [(source, source ^ mask) for source in range(groups)])


def one_hot(rows, columns, row_offset, of_column):
    row_ids = lax.broadcasted_iota(jnp.int32, (rows, columns), 0)
    column_ids = lax.broadcasted_iota(jnp.int32, (rows, columns), 1)
    return (row_ids == row_offset + of_column(column_ids)).astype(BF16)


def pack_kernel(half_ref, spectra_ref, bins_ref, alive_ref, send_ref, keep_ref, scaled_ref):
    block, width, columns = spectra_ref.shape
    freq_len = columns // 2
    tiles = freq_len // 2 // LANES
    values = spectra_ref[...].astype(F32)
    powers = jnp.mean(values * values, axis=-1, keepdims=True)
    scaled_ref[...] = values * (lax.rsqrt(powers + 1e-06) * alive_ref[...])
    half = half_ref[0]
    for tile in range(tiles):
        for window in range(width):
            for part in range(2):
                plane = (tile * width + window) * 2 + part
                base = part * freq_len + tile * LANES
                mine = pl.multiple_of(base + half * (freq_len // 2), LANES)
                other = pl.multiple_of(base + (1 - half) * (freq_len // 2), LANES)
                kept = scaled_ref[:, window, pl.ds(mine, LANES)]
                keep_ref[plane] = kept.astype(BF16).astype(F32)
                send_ref[plane] = scaled_ref[:, window, pl.ds(other, LANES)].astype(BF16)
    rounds = bins_ref.shape[0]
    plane = jnp.zeros((block, LANES), F32)
    for round_no in range(rounds):
        place = one_hot(block, LANES, -block * round_no, lambda ids: ids)
        plane = plane + jnp.dot(bins_ref[round_no].astype(F32).astype(BF16), place, preferred_element_type=F32)
    send_ref[send_ref.shape[0] - 1] = plane.astype(BF16)


def pack(half, spectra, bins, alive):
    block, width, columns = spectra.shape
    planes = columns // 2 // LANES * width
    return pl.pallas_call(
        pack_kernel,
        out_shape=(
            jax.ShapeDtypeStruct((planes + 1, block, LANES), BF16),
            jax.ShapeDtypeStruct((planes, block, LANES), F32),
        ),
        in_specs=[pl.BlockSpec(memory_space=pltpu.SMEM)] + [pl.BlockSpec(memory_space=pltpu.VMEM)] * 3,
        out_specs=(pl.BlockSpec(memory_space=pltpu.VMEM),) * 2,
        scratch_shapes=[pltpu.VMEM((block, width, columns), F32)],
        compiler_params=pltpu.CompilerParams(vmem_limit_bytes=VMEM_LIMIT),
        name="pack",
    )(half, spectra, bins, alive)


def hot_pairs(mine, theirs, round_no, block):
    pairs = block * block
    base = block * round_no
    rows = lax.broadcasted_iota(jnp.int32, (block, pairs), 0)
    columns = lax.broadcasted_iota(jnp.int32, (block, pairs), 1)
    by_second = jnp.dot(mine, one_hot(LANES, pairs, base, lambda ids: ids % block), preferred_element_type=F32)
    by_first = jnp.dot(theirs, one_hot(LANES, pairs, base, lambda ids: ids // block), preferred_element_type=F32)
    first = jnp.sum(jnp.where(rows == columns // block, by_second, 0.0), axis=0, keepdims=True)
    second = jnp.sum(jnp.where(rows == columns % block, by_first, 0.0), axis=0, keepdims=True)
    bin_ids = lax.broadcasted_iota(jnp.int32, (NB, pairs), 0).astype(F32)
    hot_first = (bin_ids == first).astype(F32)
    hot_second = (bin_ids == second).astype(F32)
    return (hot_first + hot_second).astype(BF16), (hot_first - hot_second).astype(BF16)


def round_kernel(round_no, groups, keep_ref, send_ref, got_ref, total_ref, out_ref, plus_ref, minus_ref, real_ref, imag_ref):
    planes, block, _ = keep_ref.shape
    width = real_ref.shape[0] * groups
    tiles = planes // (2 * width)
    rows = 16
    plus, minus = hot_pairs(send_ref[planes], got_ref[planes], round_no, block)
    plus_ref[...] = plus
    minus_ref[...] = minus

    def of_channel(channel, carry):
        for tile in range(tiles):
            ones = [
                jnp.broadcast_to(keep_ref[tile * 2 * width + k, pl.ds(channel, 1), :], (rows, LANES)).astype(BF16)
                for k in range(2 * width)
            ]
            lanes = slice(tile * LANES, (tile + 1) * LANES)
            for start in range(0, block, rows):
                twos = [got_ref[tile * 2 * width + k, start : start + rows, :] for k in range(2 * width)]
                at = pl.ds(pl.multiple_of(channel * block + start, rows), rows)
                for part in range(width // groups):
                    real, imag = None, None
                    for window in range(part * groups, (part + 1) * groups):
                        one_real, one_imag = ones[2 * window], ones[2 * window + 1]
                        two_real, two_imag = twos[2 * window], twos[2 * window + 1]
                        more_real = one_real * two_real + one_imag * two_imag
                        more_imag = one_imag * two_real - one_real * two_imag
                        real = more_real if real is None else real + more_real
                        imag = more_imag if imag is None else imag + more_imag
                    real_ref[part, at, lanes] = real
                    imag_ref[part, at, lanes] = imag
        return carry

    lax.fori_loop(0, block, of_channel, 0)
    half = tiles * LANES
    real = total_ref[:, :half].astype(F32)
    imag = total_ref[:, half:].astype(F32)
    for part in range(width // groups):
        real = real + jnp.dot(plus_ref[...], real_ref[part], preferred_element_type=F32)
        imag = imag + jnp.dot(minus_ref[...], imag_ref[part], preferred_element_type=F32)
    out_ref[:, :half] = real.astype(out_ref.dtype)
    out_ref[:, half:] = imag.astype(out_ref.dtype)


def add_round(round_no, width, keep, send, got, total, out_dtype, groups=2):
    planes, block, _ = keep.shape
    half = planes // (2 * width) * LANES
    pairs = block * block
    return pl.pallas_call(
        functools.partial(round_kernel, round_no, groups),
        out_shape=jax.ShapeDtypeStruct((NB, 2 * half), out_dtype),
        in_specs=[pl.BlockSpec(memory_space=pltpu.VMEM)] * 4,
        out_specs=pl.BlockSpec(memory_space=pltpu.VMEM),
        scratch_shapes=[
            pltpu.VMEM((NB, pairs), BF16),
            pltpu.VMEM((NB, pairs), BF16),
            pltpu.VMEM((width // groups, pairs, half), BF16),
            pltpu.VMEM((width // groups, pairs, half), BF16),
        ],
        compiler_params=pltpu.CompilerParams(vmem_limit_bytes=VMEM_LIMIT),
        cost_estimate=pl.CostEstimate(flops=2 * 10**9, bytes_accessed=3 * 10**6, transcendentals=0),
        name="add_round",
    )(keep, send, got, total)


def lag_kernel(scaling, parities, parts_ref, high_ref, low_ref, out_ref):
    sums = []
    for half in range(2):
        total = None
        for source, parity in enumerate(parities):
            if parity == half:
                part = parts_ref[source].astype(F32)
                total = part if total is None else total + part
        sums.append(total)
    values = jnp.concatenate(sums, axis=1)
    high = values.astype(BF16)
    low = (values - high.astype(F32)).astype(BF16)
    table = high_ref[...]
    result = jnp.dot(high, table, preferred_element_type=F32)
    result = result + jnp.dot(low, table, preferred_element_type=F32)
    result = result + jnp.dot(high, low_ref[...], preferred_element_type=F32)
    out_ref[...] = result * scaling


def to_lags(parts, parities, scaling, high, low):
    return pl.pallas_call(
        functools.partial(lag_kernel, scaling, parities),
        out_shape=jax.ShapeDtypeStruct((parts.shape[1], LAGS), F32),
        in_specs=[pl.BlockSpec(memory_space=pltpu.VMEM)] * 3,
        out_specs=pl.BlockSpec(memory_space=pltpu.VMEM),
        compiler_params=pltpu.CompilerParams(vmem_limit_bytes=VMEM_LIMIT),
        name="to_lags",
    )(parts, high, low)


def build_table(freq_len):
    freq_ids = np.arange(freq_len).reshape(2, 1, freq_len // 2)
    lag_ids = np.arange(LAGS) - LAGS // 2
    angles = (freq_ids[..., None] * lag_ids % NT) * (2.0 * math.pi / NT)
    weights = np.where(freq_ids == 0, 1.0, 2.0)[..., None]
    table = np.concatenate([weights * np.cos(angles), -weights * np.sin(angles)], axis=1)
    table = table.reshape(2 * freq_len, LAGS).astype(np.float32)
    high = table.astype(BF16)
    return high, (table - high.astype(np.float32)).astype(BF16)


def on_device(spectra, pair_bins, dead_mask):
    block, width, columns = spectra.shape
    freq_len = columns // 2
    groups = lax.axis_size("row") * lax.axis_size("col")
    half = parity_of(lax.axis_index(AXES)).astype(jnp.int32)[None]
    alive = dead_mask.astype(F32)[:, None, None]
    send, keep = pack(half, spectra, pair_bins, alive)
    got = [swapped(send, round_no, groups) for round_no in range(ROUNDS)]
    total = jnp.zeros((NB, freq_len), F32)
    order = (0, 3, 1, 2)
    for round_no in order:
        last = round_no == order[-1]
        total = add_round(round_no, width, keep, send, got[round_no], total, BF16 if last else F32)
    mine = lax.all_to_all(total.reshape(groups, NB // groups, freq_len), AXES, 0, 0, tiled=True)
    pairs = ROUNDS * block * block * groups // NB
    scaling = 1.0 / (2.0 * math.sqrt(freq_len * width * pairs))
    high, low = build_table(freq_len)
    parities = [parity_of(source) for source in range(groups)]
    return to_lags(mine, parities, scaling, jnp.asarray(high), jnp.asarray(low))


def solution(mesh):
    return jax.shard_map(
        on_device,
        mesh=mesh,
        in_specs=(P(AXES, None, None), P(None, AXES, None), P(AXES)),
        out_specs=P(AXES, None),
        check_vma=False,
    )
```

time: 448 us -> 52.4 us (0.12); the launches traced: 442 us -> 52.1 us
  matrix products: 135 us -> 0 us
  local copies, waits for them, and re-layouts: 138 us -> 3.92 us
  waiting for transfers between devices: 123 us -> 7.21 us
  other arithmetic: 25.3 us -> 0.66 us
  Pallas kernels: 0 us -> 20 us
  blocking collectives: 0 us -> 13.8 us
  between operations: 13.8 us -> 0.07 us
    dot_general x21 -> x0, matrix products: 135 us -> none  [the longest x4 35 us: cross_spectra(): jnp.einsum('iwk,jwk->ijk', one_real, two_real, preferred_element_type=jnp...]
    unnamed x2 -> x0, waiting for transfers between devices: 116 us -> none
    sub x4 -> x0, local copies, waits for them, and re-layouts: 56.1 us -> none  [cross_spectra(): jnp.einsum('iwk,jwk->ijk', one_imag, two_real, preferred_element_type=jnp...]
    add x4 -> x0, local copies, waits for them, and re-layouts: 44.5 us -> none  [cross_spectra(): jnp.einsum('iwk,jwk->ijk', one_real, two_real, preferred_element_type=jnp...]
    pallas_call x0 -> x6, Pallas kernels: none -> 20 us  [the longest x4 16.3 us: add_round(): pl.pallas_call(functools.partial(round_kernel, round_no, groups), out_sha...]
    unnamed x44 -> x8, local copies, waits for them, and re-layouts: 23.3 us -> 3.76 us
    all_to_all x0 -> x1, blocking collectives: none -> 13.8 us  [on_device(): lax.all_to_all(total.reshape(groups, NB // groups, freq_len), AXES, 0, 0,...]
    mul x1 -> x0, other arithmetic: 12.6 us -> none  [build_table(): weights * jnp.cos(angles)]
  transfers between devices with their start and end apart: 5 -> 4, of which waited for: 2 -> 2; matrix products, arithmetic and copies ran while one was open for 16% -> 0% of each run, Pallas kernels for 0% -> 23%
where the time goes in v1:
time: 52.4 us; the launch traced here: 52.1 us
  Pallas kernels  20 us (38%)
  blocking collectives  13.8 us (26%)
  waiting for transfers between devices  7.21 us (14%)
  starting transfers between devices  6.4 us (12%)
  local copies, waits for them, and re-layouts  3.92 us (7%)
  other arithmetic  0.66 us (1%)
    pallas_call x4, Pallas kernels, add_round(): pl.pallas_call(functools.partial(round_kernel, round_no, groups), out_sha...  16.3 us
    all_to_all x1, blocking collectives, on_device(): lax.all_to_all(total.reshape(groups, NB // groups, freq_len), AXES, 0, 0,...  13.8 us
    ppermute x4, waiting for transfers between devices, swapped(): lax.ppermute(value, AXES, [(source, source ^ mask) for source in range(gr...  7.21 us
    ppermute x4, starting transfers between devices, swapped(): lax.ppermute(value, AXES, [(source, source ^ mask) for source in range(gr...  6.4 us
    unnamed x8, local copies, waits for them, and re-layouts  3.76 us
    pallas_call x1, Pallas kernels, pack(): pl.pallas_call(pack_kernel, out_shape=(jax.ShapeDtypeStruct((planes + 1,...  1.9 us
    pallas_call x1, Pallas kernels, to_lags(): pl.pallas_call(functools.partial(lag_kernel, scaling, parities), out_shap...  1.81 us
  transfers between devices with their start and end apart: 4, of which 2 were waited for; matrix products, arithmetic and copies ran while one was open for 0% of the time, Pallas kernels for 23%

profile of v1, /device:TPU:1, one launch (start us, length us, event | category | flops | bytes accessed | tf_op | source)
XLA Modules:
  0.0 52.1 jit_solution(1277361400060204089)
XLA Ops:
  0.0 0.7 %convert_bitcast_fusion = f32[32,1,1]{0,2,1:T(1,128)S(1)} fusion(s32[32]{0:T(128)} %param.7), kind=kLoop, calls=%fused_computation | loop fusion | flops 32 | bytes 256 | tf_op jit(solution)/shard_map/broadcast_in_dim | solution.py:209
  0.7 0.1 copy.6.alive_ref
  0.7 0.0 copy-start.2
  0.8 1.1 %copy-done.2 = bf16[32,8,1536]{2,1,0:T(8,128)(2,1)S(1)} copy-done((bf16[32,8,1536]{2,1,0:T(8,128)(2,1)S(1)}, bf16[32,8,1536]{2,1,0:T(8,128)(2,1)}, u32[]{:S(2)}) %copy-start.2) | copy-done | bytes 786456
  1.9 0.0 copy-start.3
  1.9 0.8 %copy-done.3 = s32[4,32,32]{2,1,0:T(8,128)S(1)} copy-done((s32[4,32,32]{2,1,0:T(8,128)S(1)}, s32[4,32,32]{2,1,0:T(8,128)}, u32[]{:S(2)}) %copy-start.3) | copy-done | bytes 16408
  2.7 1.9 %pack.1 = (bf16[49,32,128]{2,1,0:T(8,128)(2,1)S(1)}, f32[48,32,128]{2,1,0:T(8,128)S(1)}) custom-call(s32[1]{0:T(128)} %bitcast.half_ref, bf16[32,8,1536]{2,1,0:T(8,128)(2,1)S(1)} %copy-done.2, s32[4,32,32]{2,1,0:T(8,128)S(1)} %copy-done.3, f32[32,1,1]{2,1,0:T(1,128)S(1)} %copy.6.alive_ref), custom_call_target="tpu_custom_call" | custom-call | tf_op jit(solution)/shard_map/pack/pallas_call | solution.py:70
  4.6 0.1 collective-permute-start.3
  4.8 2.7 %collective-permute-start.2 = (bf16[49,32,128]{2,1,0:T(8,128)(2,1)S(1)}, bf16[49,32,128]{2,1,0:T(8,128)(2,1)S(1)}, u32[]{:S(2)}, u32[]{:S(2)}) collective-permute-start(bf16[49,32,128]{2,1,0:T(8,128)(2,1)S(1)} %get-tuple-element.8.send_ref), channel_id=1, source_target_pairs={{0,8},{1,9},{2,10},{3,11},{4,12},{5,13},{6,14},{7,15},{8,0},{9,1},... | collective-permute-start | bytes 1204232 | tf_op jit(solution)/shard_map/ppermute | solution.py:32
  7.4 1.3 %collective-permute-start.1 = (bf16[49,32,128]{2,1,0:T(8,128)(2,1)S(1)}, bf16[49,32,128]{2,1,0:T(8,128)(2,1)S(1)}, u32[]{:S(2)}, u32[]{:S(2)}) collective-permute-start(bf16[49,32,128]{2,1,0:T(8,128)(2,1)S(1)} %get-tuple-element.8.send_ref), channel_id=1, source_target_pairs={{0,2},{1,3},{2,0},{3,1},{4,6},{5,7},{6,4},{7,5},{8,10},{9,11},{10,... | collective-permute-start | bytes 1204232 | tf_op jit(solution)/shard_map/ppermute | solution.py:32
  8.7 2.3 %collective-permute-start = (bf16[49,32,128]{2,1,0:T(8,128)(2,1)S(1)}, bf16[49,32,128]{2,1,0:T(8,128)(2,1)S(1)}, u32[]{:S(2)}, u32[]{:S(2)}) collective-permute-start(bf16[49,32,128]{2,1,0:T(8,128)(2,1)S(1)} %get-tuple-element.8.send_ref), channel_id=1, source_target_pairs={{0,4},{1,5},{2,6},{3,7},{4,0},{5,1},{6,2},{7,3},{8,12},{9,13},{10,... | collective-permute-start | bytes 1204232 | tf_op jit(solution)/shard_map/ppermute | solution.py:32
  11.0 0.0 collective-permute-done.3.got_ref
  11.1 4.1 %add_round.4.total_ref = f32[128,768]{1,0:T(8,128)S(1)} custom-call(f32[48,32,128]{2,1,0:T(8,128)S(1)} %get-tuple-element.7.keep_ref, bf16[49,32,128]{2,1,0:T(8,128)(2,1)S(1)} %get-tuple-element.8.send_ref, bf16[49,32,128]{2,1,0:T(8,128)(2,1)S(1)} %collective-permute-done.3.got_ref, f32[128,768]{1,0:T(8,128)S(1)} %broadcast_in_dim.11.total_ref), custom_call_target="tpu_custom_call" | custom-call | flops 2000000000 | bytes 3000000 | tf_op jit(solution)/shard_map/add_round/pallas_call | solution.py:146
  15.2 1.8 %collective-permute-done.2.got_ref = bf16[49,32,128]{2,1,0:T(8,128)(2,1)S(1)} collective-permute-done((bf16[49,32,128]{2,1,0:T(8,128)(2,1)S(1)}, bf16[49,32,128]{2,1,0:T(8,128)(2,1)S(1)}, u32[]{:S(2)}, u32[]{:S(2)}) %collective-permute-start.2) | collective-permute-done | bytes 401440 | tf_op jit(solution)/shard_map/ppermute | solution.py:32
  17.0 4.1 %add_round.5.total_ref = f32[128,768]{1,0:T(8,128)S(1)} custom-call(f32[48,32,128]{2,1,0:T(8,128)S(1)} %get-tuple-element.7.keep_ref, bf16[49,32,128]{2,1,0:T(8,128)(2,1)S(1)} %get-tuple-element.8.send_ref, bf16[49,32,128]{2,1,0:T(8,128)(2,1)S(1)} %collective-permute-done.2.got_ref, f32[128,768]{1,0:T(8,128)S(1)} %add_round.4.total_ref), custom_call_target="tpu_custom_call" | custom-call | flops 2000000000 | bytes 3000000 | tf_op jit(solution)/shard_map/add_round/pallas_call | solution.py:146
  21.1 5.4 %collective-permute-done.1.got_ref = bf16[49,32,128]{2,1,0:T(8,128)(2,1)S(1)} collective-permute-done((bf16[49,32,128]{2,1,0:T(8,128)(2,1)S(1)}, bf16[49,32,128]{2,1,0:T(8,128)(2,1)S(1)}, u32[]{:S(2)}, u32[]{:S(2)}) %collective-permute-start.1) | collective-permute-done | bytes 401440 | tf_op jit(solution)/shard_map/ppermute | solution.py:32
  26.4 4.1 %add_round.6.total_ref = f32[128,768]{1,0:T(8,128)S(1)} custom-call(f32[48,32,128]{2,1,0:T(8,128)S(1)} %get-tuple-element.7.keep_ref, bf16[49,32,128]{2,1,0:T(8,128)(2,1)S(1)} %get-tuple-element.8.send_ref, bf16[49,32,128]{2,1,0:T(8,128)(2,1)S(1)} %collective-permute-done.1.got_ref, f32[128,768]{1,0:T(8,128)S(1)} %add_round.5.total_ref), custom_call_target="tpu_custom_call" | custom-call | flops 2000000000 | bytes 3000000 | tf_op jit(solution)/shard_map/add_round/pallas_call | solution.py:146
  30.5 0.0 copy-start
  30.5 0.0 collective-permute-done.got_ref
  30.6 4.1 %add_round.7 = bf16[128,768]{1,0:T(8,128)(2,1)S(1)} custom-call(f32[48,32,128]{2,1,0:T(8,128)S(1)} %get-tuple-element.7.keep_ref, bf16[49,32,128]{2,1,0:T(8,128)(2,1)S(1)} %get-tuple-element.8.send_ref, bf16[49,32,128]{2,1,0:T(8,128)(2,1)S(1)} %collective-permute-done.got_ref, f32[128,768]{1,0:T(8,128)S(1)} %add_round.6.total_ref), custom_call_target="tpu_custom_call" | custom-call | flops 2000000000 | bytes 3000000 | tf_op jit(solution)/shard_map/add_round/pallas_call | solution.py:146
  34.6 0.1 reshape.3
  34.7 13.8 %all_to_all.5.parts_ref = bf16[32,4,768]{2,1,0:T(4,128)(2,1)S(1)} all-to-all(bf16[32,4,768]{2,1,0:T(4,128)(2,1)S(1)} %reshape.3), channel_id=1, replica_groups=mesh['row'=4,'col'=8] {'row','col'}, dimensions={0} | all-to-all | bytes 393216 | tf_op jit(solution)/shard_map/all_to_all | solution.py:217
  48.5 0.0 copy-done
  48.5 0.0 copy-start.1
  48.5 1.8 %copy-done.1 = bf16[1536,896]{1,0:T(8,128)(2,1)S(1)} copy-done((bf16[1536,896]{1,0:T(8,128)(2,1)S(1)}, bf16[1536,896]{1,0:T(8,128)(2,1)}, u32[]{:S(2)}) %copy-start.1) | copy-done | bytes 2752536
  50.3 1.8 %to_lags.1 = f32[4,896]{1,0:T(4,128)} custom-call(bf16[32,4,768]{2,1,0:T(4,128)(2,1)S(1)} %all_to_all.5.parts_ref, bf16[1536,896]{1,0:T(8,128)(2,1)S(1)} %copy-done.1, bf16[1536,896]{1,0:T(8,128)(2,1)S(1)} %copy-done), custom_call_target="tpu_custom_call" | custom-call | tf_op jit(solution)/shard_map/to_lags/pallas_call | solution.py:183
  (1 shorter events, 0.0 us)
Async XLA Ops:
  0.7 1.1 %copy-start.2 = (bf16[32,8,1536]{2,1,0:T(8,128)(2,1)S(1)}, bf16[32,8,1536]{2,1,0:T(8,128)(2,1)}, u32[]{:S(2)}) copy-start(bf16[32,8,1536]{2,1,0:T(8,128)(2,1)} %spectra_ref.1) | copy-start | bytes 2359300
  1.9 0.8 %copy-start.3 = (s32[4,32,32]{2,1,0:T(8,128)S(1)}, s32[4,32,32]{2,1,0:T(8,128)}, u32[]{:S(2)}) copy-start(s32[4,32,32]{2,1,0:T(8,128)} %bins_ref.1) | copy-start | bytes 49156
  4.6 6.4 %collective-permute-start.3 = (bf16[49,32,128]{2,1,0:T(8,128)(2,1)S(1)}, bf16[49,32,128]{2,1,0:T(8,128)(2,1)S(1)}, u32[]{:S(2)}, u32[]{:S(2)}) collective-permute-start(bf16[49,32,128]{2,1,0:T(8,128)(2,1)S(1)} %get-tuple-element.8.send_ref), channel_id=1, source_target_pairs={{0,1},{1,0},{2,3},{3,2},{4,5},{5,4},{6,7},{7,6},{8,9},{9,8},{10,11... | collective-permute-start | bytes 1204232 | tf_op jit(solution)/shard_map/ppermute | solution.py:32
  4.8 12.2 %collective-permute-start.2 = (bf16[49,32,128]{2,1,0:T(8,128)(2,1)S(1)}, bf16[49,32,128]{2,1,0:T(8,128)(2,1)S(1)}, u32[]{:S(2)}, u32[]{:S(2)}) collective-permute-start(bf16[49,32,128]{2,1,0:T(8,128)(2,1)S(1)} %get-tuple-element.8.send_ref), channel_id=1, source_target_pairs={{0,8},{1,9},{2,10},{3,11},{4,12},{5,13},{6,14},{7,15},{8,0},{9,1},... | collective-permute-start | bytes 1204232 | tf_op jit(solution)/shard_map/ppermute | solution.py:32
  7.4 19.0 %collective-permute-start.1 = (bf16[49,32,128]{2,1,0:T(8,128)(2,1)S(1)}, bf16[49,32,128]{2,1,0:T(8,128)(2,1)S(1)}, u32[]{:S(2)}, u32[]{:S(2)}) collective-permute-start(bf16[49,32,128]{2,1,0:T(8,128)(2,1)S(1)} %get-tuple-element.8.send_ref), channel_id=1, source_target_pairs={{0,2},{1,3},{2,0},{3,1},{4,6},{5,7},{6,4},{7,5},{8,10},{9,11},{10,... | collective-permute-start | bytes 1204232 | tf_op jit(solution)/shard_map/ppermute | solution.py:32
  8.7 21.8 %collective-permute-start = (bf16[49,32,128]{2,1,0:T(8,128)(2,1)S(1)}, bf16[49,32,128]{2,1,0:T(8,128)(2,1)S(1)}, u32[]{:S(2)}, u32[]{:S(2)}) collective-permute-start(bf16[49,32,128]{2,1,0:T(8,128)(2,1)S(1)} %get-tuple-element.8.send_ref), channel_id=1, source_target_pairs={{0,4},{1,5},{2,6},{3,7},{4,0},{5,1},{6,2},{7,3},{8,12},{9,13},{10,... | collective-permute-start | bytes 1204232 | tf_op jit(solution)/shard_map/ppermute | solution.py:32
  30.5 18.0 %copy-start = (bf16[1536,896]{1,0:T(8,128)(2,1)S(1)}, bf16[1536,896]{1,0:T(8,128)(2,1)}, u32[]{:S(2)}) copy-start(bf16[1536,896]{1,0:T(8,128)(2,1)} %constant.34.clone.low_ref) | copy-start | bytes 8257540
  48.5 1.8 %copy-start.1 = (bf16[1536,896]{1,0:T(8,128)(2,1)S(1)}, bf16[1536,896]{1,0:T(8,128)(2,1)}, u32[]{:S(2)}) copy-start(bf16[1536,896]{1,0:T(8,128)(2,1)} %constant.33.clone.high_ref) | copy-start | bytes 8257540

commit v2 on v0

v2 whole, which is shorter than its diff:
```python
import functools
import math

import jax
import jax.numpy as jnp
import numpy as np
from jax import lax
from jax.experimental import pallas as pl
from jax.experimental.pallas import tpu as pltpu
from jax.sharding import PartitionSpec as P

NT = 1600
LAGS = 896
NB = 128
ROUNDS = 4
LANES = 128
ROWS = 16
SUMMED = 2
AXES = ("row", "col")
F32 = jnp.float32
BF16 = jnp.bfloat16
VMEM = pl.BlockSpec(memory_space=pltpu.VMEM)
HBM = pl.BlockSpec(memory_space=pltpu.MemorySpace.HBM)
LARGE = pltpu.CompilerParams(vmem_limit_bytes=63488 * 2**10)
PARAMS = pltpu.CompilerParams(vmem_limit_bytes=48 * 2**20)


def parity_of(index):
    total = 0
    for bit in range(ROUNDS):
        total = total + ((index >> bit) & 1)
    return total % 2


def half_here():
    return parity_of(lax.axis_index("row") * lax.axis_size("col") + lax.axis_index("col"))


def swapped(value, stride, groups):
    mask = 2**stride
    return lax.ppermute(value, AXES, [(source, source ^ mask) for source in range(groups)])


def one_hot(rows, columns, row_offset, of_column):
    row_ids = lax.broadcasted_iota(jnp.int32, (rows, columns), 0)
    column_ids = lax.broadcasted_iota(jnp.int32, (rows, columns), 1)
    return (row_ids == row_offset + of_column(column_ids)).astype(BF16)


def plane_of(scaled_ref, plane, block, half):
    tiles, width = scaled_ref.shape[0] // 4, scaled_ref.shape[1] // block
    tile, window, part = plane // (2 * width), plane // 2 % width, plane % 2
    return scaled_ref[2 * tiles * part + tiles * half + tile, pl.ds(window, block, stride=width), :]


def whiten_kernel(spectra_ref, bins_ref, alive_ref, *refs):
    first_ref, second_ref, whole_ref, keep_ref, scaled_ref, loaded_ref, loaded_bins_ref, loaded_alive_ref, sems = refs
    block, width, columns = spectra_ref.shape
    step = 8
    copies = [
        pltpu.make_async_copy(spectra_ref.at[pl.ds(at, step)], loaded_ref.at[pl.ds(at, step)], sems.at[at // step])
        for at in range(0, block, step)
    ]
    bins_copy = pltpu.make_async_copy(bins_ref, loaded_bins_ref, sems.at[block // step])
    alive_copy = pltpu.make_async_copy(alive_ref, loaded_alive_ref, sems.at[block // step + 1])
    for copy in [*copies, alive_copy, bins_copy]:
        copy.start()
    half = half_here()
    for channel in range(block):
        if channel % step == 0:
            copies[channel // step].wait()
        if channel == 0:
            alive_copy.wait()
        values = loaded_ref[channel].astype(F32)
        powers = jnp.mean(values * values, axis=-1, keepdims=True)
        values = values * (lax.rsqrt(powers + 1e-06) * loaded_alive_ref[channel].astype(F32))
        for tile in range(columns // LANES):
            scaled_ref[tile, channel * width : (channel + 1) * width, :] = values[:, tile * LANES : (tile + 1) * LANES]
    planes = keep_ref.shape[0] - 1
    firsts = first_ref.shape[0] - 1
    for plane in range(planes):
        sent = plane_of(scaled_ref, plane, block, 1 - half).astype(BF16)
        whole_ref[plane] = sent
        if plane < firsts:
            first_ref[plane] = sent
        else:
            second_ref[plane - firsts] = sent
        keep_ref[plane] = plane_of(scaled_ref, plane, block, half).astype(BF16).astype(F32)
    bins_copy.wait()
    bins = jnp.zeros((block, LANES), F32)
    for round_no in range(bins_ref.shape[0]):
        place = one_hot(block, LANES, -block * round_no, lambda ids: ids)
        bins = bins + jnp.dot(loaded_bins_ref[round_no].astype(F32).astype(BF16), place, preferred_element_type=F32)
    whole_ref[planes] = bins.astype(BF16)
    keep_ref[planes] = bins
    first_ref[firsts] = bins.astype(BF16)


def whiten(spectra, bins, alive, first_tiles):
    block, width, columns = spectra.shape
    planes = columns // 2 // LANES * width
    firsts = first_tiles * 2 * width

    def sent(count):
        return jax.ShapeDtypeStruct((count, block, LANES), BF16)

    return pl.pallas_call(
        whiten_kernel,
        out_shape=(
            sent(firsts + 1),
            sent(planes - firsts),
            sent(planes + 1),
            jax.ShapeDtypeStruct((planes + 1, block, LANES), F32),
        ),
        in_specs=[HBM, HBM, HBM],
        out_specs=(VMEM,) * 4,
        scratch_shapes=[
            pltpu.VMEM((columns // LANES, block * width, LANES), F32),
            pltpu.VMEM(spectra.shape, BF16),
            pltpu.VMEM(bins.shape, jnp.int32),
            pltpu.SMEM(alive.shape, jnp.int32),
            pltpu.SemaphoreType.DMA((block // 8 + 2,)),
        ],
        compiler_params=LARGE,
        name="whiten",
    )(spectra, bins, alive)


def hot_pairs(mine, theirs, round_no, block):
    pairs = block * block
    base = block * round_no
    rows = lax.broadcasted_iota(jnp.int32, (block, pairs), 0)
    columns = lax.broadcasted_iota(jnp.int32, (block, pairs), 1)
    by_second = jnp.dot(mine, one_hot(LANES, pairs, base, lambda ids: ids % block), preferred_element_type=F32)
    by_first = jnp.dot(theirs, one_hot(LANES, pairs, base, lambda ids: ids // block), preferred_element_type=F32)
    first = jnp.sum(jnp.where(rows == columns // block, by_second, 0.0), axis=0, keepdims=True)
    second = jnp.sum(jnp.where(rows == columns % block, by_first, 0.0), axis=0, keepdims=True)
    bin_ids = lax.broadcasted_iota(jnp.int32, (NB, pairs), 0).astype(F32).astype(BF16)
    one, zero = jnp.ones((NB, pairs), BF16), jnp.zeros((NB, pairs), BF16)
    hot_first = jnp.where(bin_ids == jnp.broadcast_to(first.astype(BF16), (NB, pairs)), one, zero)
    hot_second = jnp.where(bin_ids == jnp.broadcast_to(second.astype(BF16), (NB, pairs)), one, zero)
    return hot_first + hot_second, hot_first - hot_second


def products(keep_ref, gots, cross_ref, width, here):
    block = keep_ref.shape[1]

    def of_channel(channel, carry):
        ones = [
            jnp.broadcast_to(keep_ref[here + k, pl.ds(channel, 1), :], (ROWS, LANES)).astype(BF16)
            for k in range(2 * width)
        ]
        for number, (got_ref, there) in enumerate(gots):
            for start in range(0, block, ROWS):
                at = pl.ds(pl.multiple_of(channel * block + start, ROWS), ROWS)
                for some in range(width // SUMMED):
                    real, imag = None, None
                    for window in range(some * SUMMED, (some + 1) * SUMMED):
                        one_real, one_imag = ones[2 * window], ones[2 * window + 1]
                        two_real = got_ref[there + 2 * window, start : start + ROWS, :]
                        two_imag = got_ref[there + 2 * window + 1, start : start + ROWS, :]
                        more_real = one_real * two_real + one_imag * two_imag
                        more_imag = one_imag * two_real - one_real * two_imag
                        real = more_real if real is None else real + more_real
                        imag = more_imag if imag is None else imag + more_imag
                    lanes = slice(some % 2 * LANES, (some % 2 + 1) * LANES)
                    cross_ref[number, 0, some // 2, at, lanes] = real
                    cross_ref[number, 1, some // 2, at, lanes] = imag
        return carry

    lax.fori_loop(0, block, of_channel, 0, unroll=8 // len(gots))


def binned(hots_refs, cross_ref, part):
    total = None
    for number, hots_ref in enumerate(hots_refs):
        for some in range(cross_ref.shape[2]):
            more = jnp.dot(hots_ref[part], cross_ref[number, part, some], preferred_element_type=F32)
            total = more if total is None else total + more
    return total[:, :LANES] + total[:, LANES:]


def table_copies(table_ref, loaded_ref, sems, start):
    rows = loaded_ref.shape[1]
    half = half_here()
    return [
        pltpu.make_async_copy(table_ref.at[half, level, pl.ds(start, rows)], loaded_ref.at[level], sems.at[level])
        for level in range(2)
    ]


def lags_of(sums, loaded_ref):
    values = jnp.concatenate(sums, axis=1)
    high = values.astype(BF16)
    low = (values - high.astype(F32)).astype(BF16)
    result = jnp.dot(high, loaded_ref[0], preferred_element_type=F32)
    result = result + jnp.dot(low, loaded_ref[0], preferred_element_type=F32)
    return result + jnp.dot(high, loaded_ref[1], preferred_element_type=F32)


def stage_kernel(plan, *refs):
    refs = iter(refs)
    take = lambda count: [next(refs) for _ in range(count)]
    (keep_ref,), got_refs = take(1), take(plan["gots"])
    hots_refs, before_refs = take(plan["hots"]), take(len(plan["before"]))
    table_ref = next(refs) if plan["full"] else None
    lags_ref = next(refs) if plan["lags"] else None
    after_refs = take(len(plan["after"]))
    out_ref = next(refs) if plan["full"] else None
    hots_refs = hots_refs + take(len(plan["rounds"]))
    cross_ref = next(refs)
    width = plan["width"]
    if plan["full"]:
        loaded_ref, sums_ref, sems = take(3)
        copies = table_copies(table_ref, loaded_ref, sems, min(plan["full"]) * 2 * LANES)
        for copy in copies:
            copy.start()
    for round_no, got_ref, hots_ref in zip(plan["rounds"], got_refs, hots_refs):
        mine, theirs = keep_ref[keep_ref.shape[0] - 1].astype(BF16), got_ref[got_ref.shape[0] - 1]
        plus, minus = hot_pairs(mine, theirs, round_no, keep_ref.shape[1])
        hots_ref[0] = plus
        hots_ref[1] = minus
    places = {tile: ref for tile, ref in zip(plan["before"], before_refs)}
    for tile, starts in plan["jobs"]:
        products(keep_ref, list(zip(got_refs, starts)), cross_ref, width, tile * 2 * width)
        to = after_refs[plan["after"].index(tile)] if tile in plan["after"] else sums_ref.at[plan["full"].index(tile)]
        for part in range(2):
            sums = binned(hots_refs, cross_ref, part)
            to[part] = sums + places[tile][part] if tile in places else sums
        places[tile] = to
    if plan["full"]:
        sums = [places[tile][part] for tile in plan["full"] for part in range(2)]
        for copy in copies:
            copy.wait()
        lags = lags_of(sums, loaded_ref)
        if lags_ref is not None:
            lags = lags + lags_ref[...]
        out_ref[...] = lags.astype(out_ref.dtype)


def stage(width, keep, gots, hots, rounds, jobs, before, full=(), table=None, lags=None, lags_type=F32):
    block = keep.shape[1]
    pairs = block * block
    after = [tile for tile, _ in jobs if tile not in full]
    plan = {
        "width": width,
        "gots": len(gots),
        "hots": len(hots),
        "rounds": rounds,
        "jobs": jobs,
        "before": list(before),
        "after": after,
        "full": list(full),
        "lags": lags is not None,
    }
    out = [jax.ShapeDtypeStruct((2, NB, LANES), F32)] * len(after)
    scratch = [pltpu.VMEM((len(gots), 2, width // SUMMED // 2, pairs, 2 * LANES), BF16)]
    inputs = [keep, *gots, *hots, *before.values()]
    specs = [VMEM] * len(inputs)
    if full:
        inputs, specs = inputs + [table], specs + [HBM]
        out.append(jax.ShapeDtypeStruct((NB, LAGS), lags_type))
        scratch += [
            pltpu.VMEM((2, len(full) * 2 * LANES, LAGS), BF16),
            pltpu.VMEM((len(full), 2, NB, LANES), F32),
            pltpu.SemaphoreType.DMA((2,)),
        ]
    if lags is not None:
        inputs, specs = inputs + [lags], specs + [VMEM]
    out += [jax.ShapeDtypeStruct((2, NB, pairs), BF16)] * len(rounds)
    results = pl.pallas_call(
        functools.partial(stage_kernel, plan),
        out_shape=out,
        in_specs=specs,
        out_specs=[VMEM] * len(out),
        scratch_shapes=scratch,
        compiler_params=PARAMS,
        name="stage",
    )(*inputs)
    count = len(after)
    lags_out = results[count] if full else None
    return dict(zip(after, results)), list(results[count + bool(full) :]), lags_out


def sum_kernel(scaling, parts_ref, out_ref):
    total = parts_ref[0].astype(F32)
    for source in range(1, parts_ref.shape[0]):
        total = total + parts_ref[source].astype(F32)
    out_ref[...] = total * scaling


def summed(parts, scaling):
    return pl.pallas_call(
        functools.partial(sum_kernel, scaling),
        out_shape=jax.ShapeDtypeStruct(parts.shape[1:], F32),
        in_specs=[VMEM],
        out_specs=VMEM,
        compiler_params=PARAMS,
        name="summed",
    )(parts)


def build_table(freq_len):
    freq_ids = np.arange(freq_len).reshape(2, freq_len // 2 // LANES, 1, LANES)
    lag_ids = np.arange(LAGS) - LAGS // 2
    angles = (freq_ids[..., None] * lag_ids % NT) * (2.0 * math.pi / NT)
    weights = np.where(freq_ids == 0, 1.0, 2.0)[..., None]
    table = np.concatenate([weights * np.cos(angles), -weights * np.sin(angles)], axis=2)
    table = table.reshape(2, freq_len, LAGS).astype(np.float32)
    high = table.astype(BF16)
    return np.stack([high, (table - high.astype(np.float32)).astype(BF16)], axis=1)


def on_device(spectra, pair_bins, dead_mask):
    block, width, columns = spectra.shape
    freq_len = columns // 2
    groups = lax.axis_size("row") * lax.axis_size("col")
    table = jnp.asarray(build_table(freq_len))
    tile_planes = 2 * width

    def send(value, round_no):
        return swapped(value, round_no, groups)

    first, second, whole, keep = whiten(spectra, pair_bins, dead_mask, 2)
    core, across, far_first, near_first = send(whole, 0), send(whole, 3), send(first, 2), send(first, 1)
    far_second, near_second = send(second, 2), send(second, 1)
    work = functools.partial(stage, width, keep)
    jobs = [(tile, (tile * tile_planes,)) for tile in range(3)]
    sums, _, _ = work([core], [], [0], jobs, {})
    sums, _, _ = work([across], [], [3], jobs, sums)
    jobs = [(tile, (tile * tile_planes,) * 2) for tile in range(2)]
    _, hots, lags = work([far_first, near_first], [], [2, 1], jobs, {0: sums[0], 1: sums[1]}, (0, 1), table)
    _, _, lags = work([far_second, near_second], hots, [], [(2, (0, 0))], {2: sums[2]}, (2,), table, lags, BF16)
    mine = lax.all_to_all(lags.reshape(groups, NB // groups, LAGS), AXES, 0, 0, tiled=True)
    pairs = ROUNDS * block * block * groups // NB
    return summed(mine, 1.0 / (2.0 * math.sqrt(freq_len * width * pairs)))


def solution(mesh):
    return jax.shard_map(
        on_device,
        mesh=mesh,
        in_specs=(P(AXES, None, None), P(None, AXES, None), P(AXES)),
        out_specs=P(AXES, None),
        check_vma=False,
    )
```

time: 448 us -> 45.9 us (0.10); the launches traced: 442 us -> 45.7 us
  local copies, waits for them, and re-layouts: 138 us -> 1.2 us
  matrix products: 135 us -> 0 us
  waiting for transfers between devices: 123 us -> 1.28 us
  other arithmetic: 25.3 us -> 0 us
  Pallas kernels: 0 us -> 20.4 us
  blocking collectives: 0 us -> 16.2 us
  between operations: 13.8 us -> 0.04 us
    dot_general x21 -> x0, matrix products: 135 us -> none  [the longest x4 35 us: cross_spectra(): jnp.einsum('iwk,jwk->ijk', one_real, two_real, preferred_element_type=jnp...]
    unnamed x2 -> x0, waiting for transfers between devices: 116 us -> none
    sub x4 -> x0, local copies, waits for them, and re-layouts: 56.1 us -> none  [cross_spectra(): jnp.einsum('iwk,jwk->ijk', one_imag, two_real, preferred_element_type=jnp...]
    add x4 -> x0, local copies, waits for them, and re-layouts: 44.5 us -> none  [cross_spectra(): jnp.einsum('iwk,jwk->ijk', one_real, two_real, preferred_element_type=jnp...]
    unnamed x44 -> x2, local copies, waits for them, and re-layouts: 23.3 us -> 1.14 us
    pallas_call x0 -> x6, Pallas kernels: none -> 20.4 us  [the longest x4 16.7 us: stage(): pl.pallas_call(functools.partial(stage_kernel, plan), out_shape=out, in_s...]
    all_to_all x0 -> x1, blocking collectives: none -> 16.2 us  [on_device(): lax.all_to_all(lags.reshape(groups, NB // groups, LAGS), AXES, 0, 0, tile...]
    mul x1 -> x0, other arithmetic: 12.6 us -> none  [build_table(): weights * jnp.cos(angles)]
  transfers between devices with their start and end apart: 5 -> 6, of which waited for: 2 -> 3; matrix products, arithmetic and copies ran while one was open for 16% -> 0% of each run, Pallas kernels for 0% -> 31%
where the time goes in v2:
time: 45.9 us; the launch traced here: 45.7 us
  Pallas kernels  20.4 us (44%)
  blocking collectives  16.2 us (35%)
  starting transfers between devices  6.63 us (14%)
  waiting for transfers between devices  1.28 us (3%)
  local copies, waits for them, and re-layouts  1.2 us (3%)
    pallas_call x4, Pallas kernels, stage(): pl.pallas_call(functools.partial(stage_kernel, plan), out_shape=out, in_s...  16.7 us
    all_to_all x1, blocking collectives, on_device(): lax.all_to_all(lags.reshape(groups, NB // groups, LAGS), AXES, 0, 0, tile...  16.2 us
    ppermute x6, starting transfers between devices, swapped(): lax.ppermute(value, AXES, [(source, source ^ mask) for source in range(gr...  6.63 us
    pallas_call x1, Pallas kernels, whiten(): pl.pallas_call(whiten_kernel, out_shape=(sent(firsts + 1), sent(planes -...  3.1 us
    ppermute x6, waiting for transfers between devices, swapped(): lax.ppermute(value, AXES, [(source, source ^ mask) for source in range(gr...  1.28 us
    unnamed x2, local copies, waits for them, and re-layouts  1.14 us
  transfers between devices with their start and end apart: 6, of which 3 were waited for; matrix products, arithmetic and copies ran while one was open for 0% of the time, Pallas kernels for 31%

profile of v2, /device:TPU:1, one launch (start us, length us, event | category | flops | bytes accessed | tf_op | source)
XLA Modules:
  0.0 45.7 jit_solution(2752489259698299870)
XLA Ops:
  0.0 3.1 %whiten.1 = (bf16[33,32,128]{2,1,0:T(8,128)(2,1)}, bf16[16,32,128]{2,1,0:T(8,128)(2,1)}, bf16[49,32,128]{2,1,0:T(8,128)(2,1)}, f32[49,32,128]{2,1,0:T(8,128)}) custom-call(bf16[32,8,1536]{2,1,0:T(8,128)(2,1)} %spectra_ref.1, s32[4,32,32]{2,1,0:T(8,128)} %bins_ref.1, s32[32]{0:T(128)} %alive_ref.1), custom_call_target="tpu_custom_call" | custom-call | tf_op jit(solution)/shard_map/whiten/pallas_call | solution.py:107
  3.1 0.1 collective-permute-start.5
  3.2 2.7 %collective-permute-start.4 = (bf16[49,32,128]{2,1,0:T(8,128)(2,1)}, bf16[49,32,128]{2,1,0:T(8,128)(2,1)S(1)}, u32[]{:S(2)}, u32[]{:S(2)}) collective-permute-start(bf16[49,32,128]{2,1,0:T(8,128)(2,1)} %get-tuple-element.21), channel_id=1, source_target_pairs={{0,8},{1,9},{2,10},{3,11},{4,12},{5,13},{6,14},{7,15},{8,0},{9,1},... | collective-permute-start | bytes 1204232 | tf_op jit(solution)/shard_map/ppermute | solution.py:41
  5.9 2.3 %collective-permute-start.2 = (bf16[33,32,128]{2,1,0:T(8,128)(2,1)}, bf16[33,32,128]{2,1,0:T(8,128)(2,1)S(1)}, u32[]{:S(2)}, u32[]{:S(2)}) collective-permute-start(bf16[33,32,128]{2,1,0:T(8,128)(2,1)} %get-tuple-element.20), channel_id=1, source_target_pairs={{0,4},{1,5},{2,6},{3,7},{4,0},{5,1},{6,2},{7,3},{8,12},{9,13},{10,... | collective-permute-start | bytes 811016 | tf_op jit(solution)/shard_map/ppermute | solution.py:41
  8.2 1.3 %collective-permute-start.3 = (bf16[33,32,128]{2,1,0:T(8,128)(2,1)}, bf16[33,32,128]{2,1,0:T(8,128)(2,1)S(1)}, u32[]{:S(2)}, u32[]{:S(2)}) collective-permute-start(bf16[33,32,128]{2,1,0:T(8,128)(2,1)} %get-tuple-element.20), channel_id=1, source_target_pairs={{0,2},{1,3},{2,0},{3,1},{4,6},{5,7},{6,4},{7,5},{8,10},{9,11},{10,... | collective-permute-start | bytes 811016 | tf_op jit(solution)/shard_map/ppermute | solution.py:41
  9.5 0.1 collective-permute-start
  9.6 0.0 collective-permute-done.5.refs_1_
  9.6 0.2 collective-permute-start.1
  9.7 0.0 copy-start
  9.7 1.1 %copy-done = f32[49,32,128]{2,1,0:T(8,128)S(1)} copy-done((f32[49,32,128]{2,1,0:T(8,128)S(1)}, f32[49,32,128]{2,1,0:T(8,128)}, u32[]{:S(2)}) %copy-start) | copy-done | bytes 802840
  10.9 4.2 %stage.4 = (f32[2,128,128]{2,1,0:T(8,128)S(1)}, f32[2,128,128]{2,1,0:T(8,128)S(1)}, f32[2,128,128]{2,1,0:T(8,128)S(1)}, bf16[2,128,1024]{2,1,0:T(8,128)(2,1)}) custom-call(f32[49,32,128]{2,1,0:T(8,128)S(1)} %copy-done, bf16[49,32,128]{2,1,0:T(8,128)(2,1)S(1)} %collective-permute-done.5.refs_1_), custom_call_target="tpu_custom_call" | custom-call | tf_op jit(solution)/shard_map/stage/pallas_call | solution.py:271
  15.1 0.6 %collective-permute-done.4.refs_1_ = bf16[49,32,128]{2,1,0:T(8,128)(2,1)S(1)} collective-permute-done((bf16[49,32,128]{2,1,0:T(8,128)(2,1)}, bf16[49,32,128]{2,1,0:T(8,128)(2,1)S(1)}, u32[]{:S(2)}, u32[]{:S(2)}) %collective-permute-start.4) | collective-permute-done | bytes 401440 | tf_op jit(solution)/shard_map/ppermute | solution.py:41
  15.7 4.3 %stage.5 = (f32[2,128,128]{2,1,0:T(8,128)S(1)}, f32[2,128,128]{2,1,0:T(8,128)S(1)}, f32[2,128,128]{2,1,0:T(8,128)S(1)}, bf16[2,128,1024]{2,1,0:T(8,128)(2,1)}) custom-call(f32[49,32,128]{2,1,0:T(8,128)S(1)} %copy-done, bf16[49,32,128]{2,1,0:T(8,128)(2,1)S(1)} %collective-permute-done.4.refs_1_, f32[2,128,128]{2,1,0:T(8,128)S(1)} %get-tuple-element.22.refs_2_, ...), custom_call_target="tpu_custom_call" | custom-call | tf_op jit(solution)/shard_map/stage/pallas_call | solution.py:271
  20.0 0.6 %collective-permute-done.2.refs_1_ = bf16[33,32,128]{2,1,0:T(8,128)(2,1)S(1)} collective-permute-done((bf16[33,32,128]{2,1,0:T(8,128)(2,1)}, bf16[33,32,128]{2,1,0:T(8,128)(2,1)S(1)}, u32[]{:S(2)}, u32[]{:S(2)}) %collective-permute-start.2) | collective-permute-done | bytes 270368 | tf_op jit(solution)/shard_map/ppermute | solution.py:41
  20.6 0.0 collective-permute-done.3.refs_2_
  20.6 5.5 %stage.6 = (f32[128,896]{1,0:T(8,128)S(1)}, bf16[2,128,1024]{2,1,0:T(8,128)(2,1)S(1)}, bf16[2,128,1024]{2,1,0:T(8,128)(2,1)S(1)}) custom-call(f32[49,32,128]{2,1,0:T(8,128)S(1)} %copy-done, bf16[33,32,128]{2,1,0:T(8,128)(2,1)S(1)} %collective-permute-done.2.refs_1_, bf16[33,32,128]{2,1,0:T(8,128)(2,1)S(1)} %collective-permute-done.3.refs_2_, ...), custom_call_target="tpu_custom_call" | custom-call | tf_op jit(solution)/shard_map/stage/pallas_call | solution.py:271
  26.1 0.1 collective-permute-done.refs_1_
  26.2 0.0 collective-permute-done.1.refs_2_
  26.2 2.6 %stage.7 = bf16[128,896]{1,0:T(8,128)(2,1)S(1)} custom-call(f32[49,32,128]{2,1,0:T(8,128)S(1)} %copy-done, bf16[16,32,128]{2,1,0:T(8,128)(2,1)S(1)} %collective-permute-done.refs_1_, bf16[16,32,128]{2,1,0:T(8,128)(2,1)S(1)} %collective-permute-done.1.refs_2_, bf16[2,128,1024]{2,1,0:T(8,128)(2,1)S(1)} %get-tuple-element.27.refs_3_, ...), custom_call_target="tpu_custom_call" | custom-call | tf_op jit(solution)/shard_map/stage/pallas_call | solution.py:271
  28.8 0.1 reshape.3
  28.9 16.2 %all_to_all.5.parts_ref = bf16[32,4,896]{2,1,0:T(4,128)(2,1)S(1)} all-to-all(bf16[32,4,896]{2,1,0:T(4,128)(2,1)S(1)} %reshape.3), channel_id=1, replica_groups=mesh['row'=4,'col'=8] {'row','col'}, dimensions={0} | all-to-all | bytes 458752 | tf_op jit(solution)/shard_map/all_to_all | solution.py:334
  45.1 0.7 %summed.1 = f32[4,896]{1,0:T(4,128)} custom-call(bf16[32,4,896]{2,1,0:T(4,128)(2,1)S(1)} %all_to_all.5.parts_ref), custom_call_target="tpu_custom_call" | custom-call | tf_op jit(solution)/shard_map/summed/pallas_call | solution.py:293
Async XLA Ops:
  3.1 6.5 %collective-permute-start.5 = (bf16[49,32,128]{2,1,0:T(8,128)(2,1)}, bf16[49,32,128]{2,1,0:T(8,128)(2,1)S(1)}, u32[]{:S(2)}, u32[]{:S(2)}) collective-permute-start(bf16[49,32,128]{2,1,0:T(8,128)(2,1)} %get-tuple-element.21), channel_id=1, source_target_pairs={{0,1},{1,0},{2,3},{3,2},{4,5},{5,4},{6,7},{7,6},{8,9},{9,8},{10,11... | collective-permute-start | bytes 1204232 | tf_op jit(solution)/shard_map/ppermute | solution.py:41
  3.2 12.5 %collective-permute-start.4 = (bf16[49,32,128]{2,1,0:T(8,128)(2,1)}, bf16[49,32,128]{2,1,0:T(8,128)(2,1)S(1)}, u32[]{:S(2)}, u32[]{:S(2)}) collective-permute-start(bf16[49,32,128]{2,1,0:T(8,128)(2,1)} %get-tuple-element.21), channel_id=1, source_target_pairs={{0,8},{1,9},{2,10},{3,11},{4,12},{5,13},{6,14},{7,15},{8,0},{9,1},... | collective-permute-start | bytes 1204232 | tf_op jit(solution)/shard_map/ppermute | solution.py:41
  5.9 14.7 %collective-permute-start.2 = (bf16[33,32,128]{2,1,0:T(8,128)(2,1)}, bf16[33,32,128]{2,1,0:T(8,128)(2,1)S(1)}, u32[]{:S(2)}, u32[]{:S(2)}) collective-permute-start(bf16[33,32,128]{2,1,0:T(8,128)(2,1)} %get-tuple-element.20), channel_id=1, source_target_pairs={{0,4},{1,5},{2,6},{3,7},{4,0},{5,1},{6,2},{7,3},{8,12},{9,13},{10,... | collective-permute-start | bytes 811016 | tf_op jit(solution)/shard_map/ppermute | solution.py:41
  8.2 12.4 %collective-permute-start.3 = (bf16[33,32,128]{2,1,0:T(8,128)(2,1)}, bf16[33,32,128]{2,1,0:T(8,128)(2,1)S(1)}, u32[]{:S(2)}, u32[]{:S(2)}) collective-permute-start(bf16[33,32,128]{2,1,0:T(8,128)(2,1)} %get-tuple-element.20), channel_id=1, source_target_pairs={{0,2},{1,3},{2,0},{3,1},{4,6},{5,7},{6,4},{7,5},{8,10},{9,11},{10,... | collective-permute-start | bytes 811016 | tf_op jit(solution)/shard_map/ppermute | solution.py:41
  9.5 16.7 %collective-permute-start = (bf16[16,32,128]{2,1,0:T(8,128)(2,1)}, bf16[16,32,128]{2,1,0:T(8,128)(2,1)S(1)}, u32[]{:S(2)}, u32[]{:S(2)}) collective-permute-start(bf16[16,32,128]{2,1,0:T(8,128)(2,1)} %get-tuple-element.19), channel_id=1, source_target_pairs={{0,4},{1,5},{2,6},{3,7},{4,0},{5,1},{6,2},{7,3},{8,12},{9,13},{10,... | collective-permute-start | bytes 393224 | tf_op jit(solution)/shard_map/ppermute | solution.py:41
  9.6 16.6 %collective-permute-start.1 = (bf16[16,32,128]{2,1,0:T(8,128)(2,1)}, bf16[16,32,128]{2,1,0:T(8,128)(2,1)S(1)}, u32[]{:S(2)}, u32[]{:S(2)}) collective-permute-start(bf16[16,32,128]{2,1,0:T(8,128)(2,1)} %get-tuple-element.19), channel_id=1, source_target_pairs={{0,2},{1,3},{2,0},{3,1},{4,6},{5,7},{6,4},{7,5},{8,10},{9,11},{10,... | collective-permute-start | bytes 393224 | tf_op jit(solution)/shard_map/ppermute | solution.py:41
  9.7 1.1 %copy-start = (f32[49,32,128]{2,1,0:T(8,128)S(1)}, f32[49,32,128]{2,1,0:T(8,128)}, u32[]{:S(2)}) copy-start(f32[49,32,128]{2,1,0:T(8,128)} %get-tuple-element.18.refs_0_) | copy-start | bytes 2408452

commit v3 on v2

--- a/solution.py
+++ b/solution.py
@@ -15,6 +15,7 @@
 ROUNDS = 4
 LANES = 128
 ROWS = 16
+STEP = 16
 SUMMED = 2
 AXES = ("row", "col")
 F32 = jnp.float32
@@ -54,21 +55,21 @@
 
 
 def whiten_kernel(spectra_ref, bins_ref, alive_ref, *refs):
-    first_ref, second_ref, whole_ref, keep_ref, scaled_ref, loaded_ref, loaded_bins_ref, loaded_alive_ref, sems = refs
+    (first_ref, second_ref, whole_ref, keep_ref), refs = refs[:4], refs[4:]
+    scaled_ref, loaded_ref, loaded_bins_ref, loaded_alive_ref, sent_ref, kept_ref, sems, out_sems = refs
     block, width, columns = spectra_ref.shape
-    step = 8
     copies = [
-        pltpu.make_async_copy(spectra_ref.at[pl.ds(at, step)], loaded_ref.at[pl.ds(at, step)], sems.at[at // step])
-        for at in range(0, block, step)
+        pltpu.make_async_copy(spectra_ref.at[pl.ds(at, STEP)], loaded_ref.at[pl.ds(at, STEP)], sems.at[at // STEP])
+        for at in range(0, block, STEP)
     ]
-    bins_copy = pltpu.make_async_copy(bins_ref, loaded_bins_ref, sems.at[block // step])
-    alive_copy = pltpu.make_async_copy(alive_ref, loaded_alive_ref, sems.at[block // step + 1])
+    bins_copy = pltpu.make_async_copy(bins_ref, loaded_bins_ref, sems.at[block // STEP])
+    alive_copy = pltpu.make_async_copy(alive_ref, loaded_alive_ref, sems.at[block // STEP + 1])
     for copy in [*copies, alive_copy, bins_copy]:
         copy.start()
     half = half_here()
     for channel in range(block):
-        if channel % step == 0:
-            copies[channel // step].wait()
+        if channel % STEP == 0:
+            copies[channel // STEP].wait()
         if channel == 0:
             alive_copy.wait()
         values = loaded_ref[channel].astype(F32)
@@ -76,24 +77,33 @@
         values = values * (lax.rsqrt(powers + 1e-06) * loaded_alive_ref[channel].astype(F32))
         for tile in range(columns // LANES):
             scaled_ref[tile, channel * width : (channel + 1) * width, :] = values[:, tile * LANES : (tile + 1) * LANES]
-    planes = keep_ref.shape[0] - 1
+    planes = sent_ref.shape[0] - 1
     firsts = first_ref.shape[0] - 1
-    for plane in range(planes):
-        sent = plane_of(scaled_ref, plane, block, 1 - half).astype(BF16)
-        whole_ref[plane] = sent
-        if plane < firsts:
-            first_ref[plane] = sent
-        else:
-            second_ref[plane - firsts] = sent
-        keep_ref[plane] = plane_of(scaled_ref, plane, block, half).astype(BF16).astype(F32)
+    going = []
+
+    def go(source, target):
+        going.append(pltpu.make_async_copy(source, target, out_sems.at[len(going)]))
+        going[-1].start()
+
     bins_copy.wait()
     bins = jnp.zeros((block, LANES), F32)
     for round_no in range(bins_ref.shape[0]):
         place = one_hot(block, LANES, -block * round_no, lambda ids: ids)
         bins = bins + jnp.dot(loaded_bins_ref[round_no].astype(F32).astype(BF16), place, preferred_element_type=F32)
-    whole_ref[planes] = bins.astype(BF16)
-    keep_ref[planes] = bins
-    first_ref[firsts] = bins.astype(BF16)
+    sent_ref[planes] = bins.astype(BF16)
+    kept_ref[planes] = bins.astype(BF16)
+    for plane in range(planes):
+        sent_ref[plane] = plane_of(scaled_ref, plane, block, 1 - half).astype(BF16)
+        if plane == firsts - 1:
+            go(sent_ref.at[pl.ds(0, firsts)], first_ref.at[pl.ds(0, firsts)])
+            go(sent_ref.at[pl.ds(planes, 1)], first_ref.at[pl.ds(firsts, 1)])
+    go(sent_ref, whole_ref)
+    go(sent_ref.at[pl.ds(firsts, planes - firsts)], second_ref)
+    for plane in range(planes):
+        kept_ref[plane] = plane_of(scaled_ref, plane, block, half).astype(BF16)
+    go(kept_ref, keep_ref)
+    for copy in going:
+        copy.wait()
 
 
 def whiten(spectra, bins, alive, first_tiles):
@@ -106,20 +116,18 @@
 
     return pl.pallas_call(
         whiten_kernel,
-        out_shape=(
-            sent(firsts + 1),
-            sent(planes - firsts),
-            sent(planes + 1),
-            jax.ShapeDtypeStruct((planes + 1, block, LANES), F32),
-        ),
+        out_shape=(sent(firsts + 1), sent(planes - firsts), sent(planes + 1), sent(planes + 1)),
         in_specs=[HBM, HBM, HBM],
-        out_specs=(VMEM,) * 4,
+        out_specs=(HBM,) * 4,
         scratch_shapes=[
             pltpu.VMEM((columns // LANES, block * width, LANES), F32),
             pltpu.VMEM(spectra.shape, BF16),
             pltpu.VMEM(bins.shape, jnp.int32),
             pltpu.SMEM(alive.shape, jnp.int32),
-            pltpu.SemaphoreType.DMA((block // 8 + 2,)),
+            pltpu.VMEM((planes + 1, block, LANES), BF16),
+            pltpu.VMEM((planes + 1, block, LANES), BF16),
+            pltpu.SemaphoreType.DMA((block // STEP + 2,)),
+            pltpu.SemaphoreType.DMA((5,)),
         ],
         compiler_params=LARGE,
         name="whiten",
@@ -207,7 +215,11 @@
     lags_ref = next(refs) if plan["lags"] else None
     after_refs = take(len(plan["after"]))
     out_ref = next(refs) if plan["full"] else None
+    wide_ref = next(refs) if plan["widens"] else None
     hots_refs = hots_refs + take(len(plan["rounds"]))
+    if plan["widens"]:
+        wide_ref[...] = keep_ref[...].astype(F32)
+        keep_ref = wide_ref
     cross_ref = next(refs)
     width = plan["width"]
     if plan["full"]:
@@ -238,7 +250,7 @@
         out_ref[...] = lags.astype(out_ref.dtype)
 
 
-def stage(width, keep, gots, hots, rounds, jobs, before, full=(), table=None, lags=None, lags_type=F32):
+def stage(width, keep, gots, hots, rounds, jobs, before, full=(), table=None, lags=None, lags_type=F32, gives_hots=False):
     block = keep.shape[1]
     pairs = block * block
     after = [tile for tile, _ in jobs if tile not in full]
@@ -252,6 +264,7 @@
         "after": after,
         "full": list(full),
         "lags": lags is not None,
+        "widens": keep.dtype != F32,
     }
     out = [jax.ShapeDtypeStruct((2, NB, LANES), F32)] * len(after)
     scratch = [pltpu.VMEM((len(gots), 2, width // SUMMED // 2, pairs, 2 * LANES), BF16)]
@@ -267,7 +280,12 @@
         ]
     if lags is not None:
         inputs, specs = inputs + [lags], specs + [VMEM]
-    out += [jax.ShapeDtypeStruct((2, NB, pairs), BF16)] * len(rounds)
+    if keep.dtype != F32:
+        out.append(jax.ShapeDtypeStruct(keep.shape, F32))
+    if gives_hots:
+        out += [jax.ShapeDtypeStruct((2, NB, pairs), BF16)] * len(rounds)
+    else:
+        scratch = [pltpu.VMEM((2, NB, pairs), BF16)] * len(rounds) + scratch
     results = pl.pallas_call(
         functools.partial(stage_kernel, plan),
         out_shape=out,
@@ -322,15 +340,20 @@
         return swapped(value, round_no, groups)
 
     first, second, whole, keep = whiten(spectra, pair_bins, dead_mask, 2)
-    core, across, far_first, near_first = send(whole, 0), send(whole, 3), send(first, 2), send(first, 1)
+    core, far_first, near_first = send(whole, 0), send(first, 2), send(first, 1)
+    across_first, across_second = send(first, 3), send(second, 3)
+
+    def planes(tiles, gots=1):
+        return [(tile, ((tile - tiles[0]) * tile_planes,) * gots) for tile in tiles]
+
+    sums, (keep,), _ = stage(width, keep, [core], [], [0], planes((0, 1, 2)), {})
+    work = functools.partial(stage, width, keep)
+    low, across_hots, _ = work([across_first], [], [3], planes((0, 1)), {0: sums[0], 1: sums[1]}, gives_hots=True)
+    high, _, _ = work([across_second], across_hots, [], planes((2,)), {2: sums[2]})
+    second, low, high = lax.optimization_barrier((second, low, high))
     far_second, near_second = send(second, 2), send(second, 1)
-    work = functools.partial(stage, width, keep)
-    jobs = [(tile, (tile * tile_planes,)) for tile in range(3)]
-    sums, _, _ = work([core], [], [0], jobs, {})
-    sums, _, _ = work([across], [], [3], jobs, sums)
-    jobs = [(tile, (tile * tile_planes,) * 2) for tile in range(2)]
-    _, hots, lags = work([far_first, near_first], [], [2, 1], jobs, {0: sums[0], 1: sums[1]}, (0, 1), table)
-    _, _, lags = work([far_second, near_second], hots, [], [(2, (0, 0))], {2: sums[2]}, (2,), table, lags, BF16)
+    _, hots, lags = work([far_first, near_first], [], [2, 1], planes((0, 1), 2), low, (0, 1), table, gives_hots=True)
+    _, _, lags = work([far_second, near_second], hots, [], planes((2,), 2), high, (2,), table, lags, BF16)
     mine = lax.all_to_all(lags.reshape(groups, NB // groups, LAGS), AXES, 0, 0, tiled=True)
     pairs = ROUNDS * block * block * groups // NB
     return summed(mine, 1.0 / (2.0 * math.sqrt(freq_len * width * pairs)))

time: 45.9 us -> 45.1 us (0.983)
  blocking collectives: 16.2 us -> 14.2 us
  starting transfers between devices: 6.63 us -> 8.56 us
  Pallas kernels: 20.4 us -> 19.4 us
    all_to_all x1, blocking collectives: 16.2 us -> 14.2 us  [on_device(): lax.all_to_all(lags.reshape(groups, NB // groups, LAGS), AXES, 0, 0, tile...]
    ppermute x6 -> x7, starting transfers between devices: 6.63 us -> 8.56 us  [swapped(): lax.ppermute(value, AXES, [(source, source ^ mask) for source in range(gr...]
    pallas_call x4 -> x5, Pallas kernels: 16.7 us -> 16.1 us  [stage(): pl.pallas_call(functools.partial(stage_kernel, plan), out_shape=out, in_s...]
    ppermute x6 -> x7, waiting for transfers between devices: 1.28 us -> 1.65 us  [swapped(): lax.ppermute(value, AXES, [(source, source ^ mask) for source in range(gr...]
  transfers between devices with their start and end apart: 6 -> 7, of which waited for: 3 -> 1; matrix products, arithmetic and copies ran while one was open for 0% -> 0% of each run, Pallas kernels for 31% -> 30%
where the time goes in v3:
time: 45.1 us; the launch traced here: 44.9 us
  Pallas kernels  19.4 us (43%)
  blocking collectives  14.2 us (31%)
  starting transfers between devices  8.56 us (19%)
  waiting for transfers between devices  1.65 us (4%)
  local copies, waits for them, and re-layouts  1.06 us (2%)
    pallas_call x5, Pallas kernels, stage(): pl.pallas_call(functools.partial(stage_kernel, plan), out_shape=out, in_s...  16.1 us
    all_to_all x1, blocking collectives, on_device(): lax.all_to_all(lags.reshape(groups, NB // groups, LAGS), AXES, 0, 0, tile...  14.2 us
    ppermute x7, starting transfers between devices, swapped(): lax.ppermute(value, AXES, [(source, source ^ mask) for source in range(gr...  8.56 us
    pallas_call x1, Pallas kernels, whiten(): pl.pallas_call(whiten_kernel, out_shape=(sent(firsts + 1), sent(planes -...  2.65 us
    ppermute x7, waiting for transfers between devices, swapped(): lax.ppermute(value, AXES, [(source, source ^ mask) for source in range(gr...  1.65 us
    unnamed x2, local copies, waits for them, and re-layouts  1 us
  transfers between devices with their start and end apart: 7, of which 1 were waited for; matrix products, arithmetic and copies ran while one was open for 0% of the time, Pallas kernels for 30%

profile of v3, /device:TPU:1, one launch (start us, length us, event | category | flops | bytes accessed | tf_op | source)
XLA Modules:
  0.0 44.9 jit_solution(14046687406427490122)
XLA Ops:
  0.0 2.6 %whiten.1 = (bf16[33,32,128]{2,1,0:T(8,128)(2,1)}, bf16[16,32,128]{2,1,0:T(8,128)(2,1)}, bf16[49,32,128]{2,1,0:T(8,128)(2,1)}, bf16[49,32,128]{2,1,0:T(8,128)(2,1)}) custom-call(bf16[32,8,1536]{2,1,0:T(8,128)(2,1)} %spectra_ref.1, s32[4,32,32]{2,1,0:T(8,128)} %bins_ref.1, s32[32]{0:T(128)} %alive_ref.1), custom_call_target="tpu_custom_call" | custom-call | tf_op jit(solution)/shard_map/whiten/pallas_call | solution.py:117
  2.7 0.1 collective-permute-start
  2.8 2.7 %collective-permute-start.1 = (bf16[33,32,128]{2,1,0:T(8,128)(2,1)}, bf16[33,32,128]{2,1,0:T(8,128)(2,1)S(1)}, u32[]{:S(2)}, u32[]{:S(2)}) collective-permute-start(bf16[33,32,128]{2,1,0:T(8,128)(2,1)} %get-tuple-element.27), channel_id=1, source_target_pairs={{0,8},{1,9},{2,10},{3,11},{4,12},{5,13},{6,14},{7,15},{8,0},{9,1},... | collective-permute-start | bytes 811016 | tf_op jit(solution)/shard_map/ppermute | solution.py:42
  5.5 2.3 %collective-permute-start.5 = (bf16[33,32,128]{2,1,0:T(8,128)(2,1)}, bf16[33,32,128]{2,1,0:T(8,128)(2,1)S(1)}, u32[]{:S(2)}, u32[]{:S(2)}) collective-permute-start(bf16[33,32,128]{2,1,0:T(8,128)(2,1)} %get-tuple-element.27), channel_id=1, source_target_pairs={{0,4},{1,5},{2,6},{3,7},{4,0},{5,1},{6,2},{7,3},{8,12},{9,13},{10,... | collective-permute-start | bytes 811016 | tf_op jit(solution)/shard_map/ppermute | solution.py:42
  7.8 1.3 %collective-permute-start.6 = (bf16[33,32,128]{2,1,0:T(8,128)(2,1)}, bf16[33,32,128]{2,1,0:T(8,128)(2,1)S(1)}, u32[]{:S(2)}, u32[]{:S(2)}) collective-permute-start(bf16[33,32,128]{2,1,0:T(8,128)(2,1)} %get-tuple-element.27), channel_id=1, source_target_pairs={{0,2},{1,3},{2,0},{3,1},{4,6},{5,7},{6,4},{7,5},{8,10},{9,11},{10,... | collective-permute-start | bytes 811016 | tf_op jit(solution)/shard_map/ppermute | solution.py:42
  9.1 0.3 collective-permute-start.2
  9.3 0.0 collective-permute-done.refs_1_
  9.3 0.0 copy-start
  9.3 1.0 %copy-done = bf16[49,32,128]{2,1,0:T(8,128)(2,1)S(1)} copy-done((bf16[49,32,128]{2,1,0:T(8,128)(2,1)S(1)}, bf16[49,32,128]{2,1,0:T(8,128)(2,1)}, u32[]{:S(2)}) %copy-start) | copy-done | bytes 401432
  10.3 4.0 %stage.5 = (f32[2,128,128]{2,1,0:T(8,128)S(1)}, f32[2,128,128]{2,1,0:T(8,128)S(1)}, f32[2,128,128]{2,1,0:T(8,128)S(1)}, f32[49,32,128]{2,1,0:T(8,128)S(1)}) custom-call(bf16[49,32,128]{2,1,0:T(8,128)(2,1)S(1)} %copy-done, bf16[49,32,128]{2,1,0:T(8,128)(2,1)S(1)} %collective-permute-done.refs_1_), custom_call_target="tpu_custom_call" | custom-call | tf_op jit(solution)/shard_map/stage/pallas_call | solution.py:289
  14.3 0.0 collective-permute-done.1.refs_1_
  14.3 2.7 %stage.6 = (f32[2,128,128]{2,1,0:T(8,128)S(1)}, f32[2,128,128]{2,1,0:T(8,128)S(1)}, bf16[2,128,1024]{2,1,0:T(8,128)(2,1)S(1)}) custom-call(f32[49,32,128]{2,1,0:T(8,128)S(1)} %get-tuple-element.25.refs_0_, bf16[33,32,128]{2,1,0:T(8,128)(2,1)S(1)} %collective-permute-done.1.refs_1_, f32[2,128,128]{2,1,0:T(8,128)S(1)} %get-tuple-element.28.refs_2_, ...), custom_call_target="tpu_custom_call" | custom-call | tf_op jit(solution)/shard_map/stage/pallas_call | solution.py:289
  17.1 0.0 collective-permute-done.2.refs_1_
  17.1 1.2 %stage.7.refs_5_ = f32[2,128,128]{2,1,0:T(8,128)S(1)} custom-call(f32[49,32,128]{2,1,0:T(8,128)S(1)} %get-tuple-element.25.refs_0_, bf16[16,32,128]{2,1,0:T(8,128)(2,1)S(1)} %collective-permute-done.2.refs_1_, bf16[2,128,1024]{2,1,0:T(8,128)(2,1)S(1)} %get-tuple-element.32.refs_2_, f32[2,128,128]{2,1,0:T(8,128)S(1)} %get-tuple-element.33.refs_3_), custom_call_target="tpu_custom_call" | custom-call | tf_op jit(solution)/shard_map/stage/pallas_call | solution.py:289
  18.3 0.6 %collective-permute-start.3 = (bf16[16,32,128]{2,1,0:T(8,128)(2,1)}, bf16[16,32,128]{2,1,0:T(8,128)(2,1)S(1)}, u32[]{:S(2)}, u32[]{:S(2)}) collective-permute-start(bf16[16,32,128]{2,1,0:T(8,128)(2,1)} %get-tuple-element.34), channel_id=1, source_target_pairs={{0,4},{1,5},{2,6},{3,7},{4,0},{5,1},{6,2},{7,3},{8,12},{9,13},{10,... | collective-permute-start | bytes 393224 | tf_op jit(solution)/shard_map/ppermute | solution.py:42
  18.9 1.3 %collective-permute-start.4 = (bf16[16,32,128]{2,1,0:T(8,128)(2,1)}, bf16[16,32,128]{2,1,0:T(8,128)(2,1)S(1)}, u32[]{:S(2)}, u32[]{:S(2)}) collective-permute-start(bf16[16,32,128]{2,1,0:T(8,128)(2,1)} %get-tuple-element.34), channel_id=1, source_target_pairs={{0,2},{1,3},{2,0},{3,1},{4,6},{5,7},{6,4},{7,5},{8,10},{9,11},{10,... | collective-permute-start | bytes 393224 | tf_op jit(solution)/shard_map/ppermute | solution.py:42
  20.2 0.0 collective-permute-done.5.refs_1_
  20.2 0.0 collective-permute-done.6.refs_2_
  20.2 5.5 %stage.8 = (f32[128,896]{1,0:T(8,128)S(1)}, bf16[2,128,1024]{2,1,0:T(8,128)(2,1)S(1)}, bf16[2,128,1024]{2,1,0:T(8,128)(2,1)S(1)}) custom-call(f32[49,32,128]{2,1,0:T(8,128)S(1)} %get-tuple-element.25.refs_0_, bf16[33,32,128]{2,1,0:T(8,128)(2,1)S(1)} %collective-permute-done.5.refs_1_, bf16[33,32,128]{2,1,0:T(8,128)(2,1)S(1)} %collective-permute-done.6.refs_2_, ...), custom_call_target="tpu_custom_call" | custom-call | tf_op jit(solution)/shard_map/stage/pallas_call | solution.py:289
  25.7 1.6 %collective-permute-done.3.refs_1_ = bf16[16,32,128]{2,1,0:T(8,128)(2,1)S(1)} collective-permute-done((bf16[16,32,128]{2,1,0:T(8,128)(2,1)}, bf16[16,32,128]{2,1,0:T(8,128)(2,1)S(1)}, u32[]{:S(2)}, u32[]{:S(2)}) %collective-permute-start.3) | collective-permute-done | bytes 131104 | tf_op jit(solution)/shard_map/ppermute | solution.py:42
  27.4 0.0 collective-permute-done.4.refs_2_
  27.4 2.6 %stage.9 = bf16[128,896]{1,0:T(8,128)(2,1)S(1)} custom-call(f32[49,32,128]{2,1,0:T(8,128)S(1)} %get-tuple-element.25.refs_0_, bf16[16,32,128]{2,1,0:T(8,128)(2,1)S(1)} %collective-permute-done.3.refs_1_, bf16[16,32,128]{2,1,0:T(8,128)(2,1)S(1)} %collective-permute-done.4.refs_2_, bf16[2,128,1024]{2,1,0:T(8,128)(2,1)S(1)} %get-tuple-element.37.refs_3_, ...), custom_call_target="tpu_custom_call" | custom-call | tf_op jit(solution)/shard_map/stage/pallas_call | solution.py:289
  30.0 0.1 reshape.3
  30.1 14.2 %all_to_all.5.parts_ref = bf16[32,4,896]{2,1,0:T(4,128)(2,1)S(1)} all-to-all(bf16[32,4,896]{2,1,0:T(4,128)(2,1)S(1)} %reshape.3), channel_id=1, replica_groups=mesh['row'=4,'col'=8] {'row','col'}, dimensions={0} | all-to-all | bytes 458752 | tf_op jit(solution)/shard_map/all_to_all | solution.py:357
  44.3 0.7 %summed.1 = f32[4,896]{1,0:T(4,128)} custom-call(bf16[32,4,896]{2,1,0:T(4,128)(2,1)S(1)} %all_to_all.5.parts_ref), custom_call_target="tpu_custom_call" | custom-call | tf_op jit(solution)/shard_map/summed/pallas_call | solution.py:311
Async XLA Ops:
  2.7 6.7 %collective-permute-start = (bf16[49,32,128]{2,1,0:T(8,128)(2,1)}, bf16[49,32,128]{2,1,0:T(8,128)(2,1)S(1)}, u32[]{:S(2)}, u32[]{:S(2)}) collective-permute-start(bf16[49,32,128]{2,1,0:T(8,128)(2,1)} %get-tuple-element.24), channel_id=1, source_target_pairs={{0,1},{1,0},{2,3},{3,2},{4,5},{5,4},{6,7},{7,6},{8,9},{9,8},{10,11... | collective-permute-start | bytes 1204232 | tf_op jit(solution)/shard_map/ppermute | solution.py:42
  2.8 11.5 %collective-permute-start.1 = (bf16[33,32,128]{2,1,0:T(8,128)(2,1)}, bf16[33,32,128]{2,1,0:T(8,128)(2,1)S(1)}, u32[]{:S(2)}, u32[]{:S(2)}) collective-permute-start(bf16[33,32,128]{2,1,0:T(8,128)(2,1)} %get-tuple-element.27), channel_id=1, source_target_pairs={{0,8},{1,9},{2,10},{3,11},{4,12},{5,13},{6,14},{7,15},{8,0},{9,1},... | collective-permute-start | bytes 811016 | tf_op jit(solution)/shard_map/ppermute | solution.py:42
  5.5 14.8 %collective-permute-start.5 = (bf16[33,32,128]{2,1,0:T(8,128)(2,1)}, bf16[33,32,128]{2,1,0:T(8,128)(2,1)S(1)}, u32[]{:S(2)}, u32[]{:S(2)}) collective-permute-start(bf16[33,32,128]{2,1,0:T(8,128)(2,1)} %get-tuple-element.27), channel_id=1, source_target_pairs={{0,4},{1,5},{2,6},{3,7},{4,0},{5,1},{6,2},{7,3},{8,12},{9,13},{10,... | collective-permute-start | bytes 811016 | tf_op jit(solution)/shard_map/ppermute | solution.py:42
  7.8 12.4 %collective-permute-start.6 = (bf16[33,32,128]{2,1,0:T(8,128)(2,1)}, bf16[33,32,128]{2,1,0:T(8,128)(2,1)S(1)}, u32[]{:S(2)}, u32[]{:S(2)}) collective-permute-start(bf16[33,32,128]{2,1,0:T(8,128)(2,1)} %get-tuple-element.27), channel_id=1, source_target_pairs={{0,2},{1,3},{2,0},{3,1},{4,6},{5,7},{6,4},{7,5},{8,10},{9,11},{10,... | collective-permute-start | bytes 811016 | tf_op jit(solution)/shard_map/ppermute | solution.py:42
  9.1 8.0 %collective-permute-start.2 = (bf16[16,32,128]{2,1,0:T(8,128)(2,1)}, bf16[16,32,128]{2,1,0:T(8,128)(2,1)S(1)}, u32[]{:S(2)}, u32[]{:S(2)}) collective-permute-start(bf16[16,32,128]{2,1,0:T(8,128)(2,1)} %get-tuple-element.34), channel_id=1, source_target_pairs={{0,8},{1,9},{2,10},{3,11},{4,12},{5,13},{6,14},{7,15},{8,0},{9,1},... | collective-permute-start | bytes 393224 | tf_op jit(solution)/shard_map/ppermute | solution.py:42
  9.3 1.0 %copy-start = (bf16[49,32,128]{2,1,0:T(8,128)(2,1)S(1)}, bf16[49,32,128]{2,1,0:T(8,128)(2,1)}, u32[]{:S(2)}) copy-start(bf16[49,32,128]{2,1,0:T(8,128)(2,1)} %get-tuple-element.23.refs_0_) | copy-start | bytes 1204228
  18.3 9.1 %collective-permute-start.3 = (bf16[16,32,128]{2,1,0:T(8,128)(2,1)}, bf16[16,32,128]{2,1,0:T(8,128)(2,1)S(1)}, u32[]{:S(2)}, u32[]{:S(2)}) collective-permute-start(bf16[16,32,128]{2,1,0:T(8,128)(2,1)} %get-tuple-element.34), channel_id=1, source_target_pairs={{0,4},{1,5},{2,6},{3,7},{4,0},{5,1},{6,2},{7,3},{8,12},{9,13},{10,... | collective-permute-start | bytes 393224 | tf_op jit(solution)/shard_map/ppermute | solution.py:42
  18.9 8.5 %collective-permute-start.4 = (bf16[16,32,128]{2,1,0:T(8,128)(2,1)}, bf16[16,32,128]{2,1,0:T(8,128)(2,1)S(1)}, u32[]{:S(2)}, u32[]{:S(2)}) collective-permute-start(bf16[16,32,128]{2,1,0:T(8,128)(2,1)} %get-tuple-element.34), channel_id=1, source_target_pairs={{0,2},{1,3},{2,0},{3,1},{4,6},{5,7},{6,4},{7,5},{8,10},{9,11},{10,... | collective-permute-start | bytes 393224 | tf_op jit(solution)/shard_map/ppermute | solution.py:42

commit v4 on v3

--- a/solution.py
+++ b/solution.py
@@ -150,7 +150,7 @@
     return hot_first + hot_second, hot_first - hot_second
 
 
-def products(keep_ref, gots, cross_ref, width, here):
+def products(keep_ref, gots, cross_ref, width, summed, here):
     block = keep_ref.shape[1]
 
     def of_channel(channel, carry):
@@ -161,9 +161,9 @@
         for number, (got_ref, there) in enumerate(gots):
             for start in range(0, block, ROWS):
                 at = pl.ds(pl.multiple_of(channel * block + start, ROWS), ROWS)
-                for some in range(width // SUMMED):
+                for some in range(width // summed):
                     real, imag = None, None
-                    for window in range(some * SUMMED, (some + 1) * SUMMED):
+                    for window in range(some * summed, (some + 1) * summed):
                         one_real, one_imag = ones[2 * window], ones[2 * window + 1]
                         two_real = got_ref[there + 2 * window, start : start + ROWS, :]
                         two_imag = got_ref[there + 2 * window + 1, start : start + ROWS, :]
@@ -176,7 +176,7 @@
                     cross_ref[number, 1, some // 2, at, lanes] = imag
         return carry
 
-    lax.fori_loop(0, block, of_channel, 0, unroll=8 // len(gots))
+    lax.fori_loop(0, block, of_channel, 0, unroll=16 // len(gots))
 
 
 def binned(hots_refs, cross_ref, part):
@@ -234,7 +234,7 @@
         hots_ref[1] = minus
     places = {tile: ref for tile, ref in zip(plan["before"], before_refs)}
     for tile, starts in plan["jobs"]:
-        products(keep_ref, list(zip(got_refs, starts)), cross_ref, width, tile * 2 * width)
+        products(keep_ref, list(zip(got_refs, starts)), cross_ref, width, plan["summed"], tile * 2 * width)
         to = after_refs[plan["after"].index(tile)] if tile in plan["after"] else sums_ref.at[plan["full"].index(tile)]
         for part in range(2):
             sums = binned(hots_refs, cross_ref, part)
@@ -250,7 +250,7 @@
         out_ref[...] = lags.astype(out_ref.dtype)
 
 
-def stage(width, keep, gots, hots, rounds, jobs, before, full=(), table=None, lags=None, lags_type=F32, gives_hots=False):
+def stage(width, keep, gots, hots, rounds, jobs, before, full=(), table=None, lags=None, lags_type=F32, gives_hots=False, summed=SUMMED):
     block = keep.shape[1]
     pairs = block * block
     after = [tile for tile, _ in jobs if tile not in full]
@@ -264,10 +264,11 @@
         "after": after,
         "full": list(full),
         "lags": lags is not None,
+        "summed": summed,
         "widens": keep.dtype != F32,
     }
     out = [jax.ShapeDtypeStruct((2, NB, LANES), F32)] * len(after)
-    scratch = [pltpu.VMEM((len(gots), 2, width // SUMMED // 2, pairs, 2 * LANES), BF16)]
+    scratch = [pltpu.VMEM((len(gots), 2, width // summed // 2, pairs, 2 * LANES), BF16)]
     inputs = [keep, *gots, *hots, *before.values()]
     specs = [VMEM] * len(inputs)
     if full:
@@ -340,7 +341,9 @@
         return swapped(value, round_no, groups)
 
     first, second, whole, keep = whiten(spectra, pair_bins, dead_mask, 2)
-    core, far_first, near_first = send(whole, 0), send(first, 2), send(first, 1)
+    core, far_first = send(whole, 0), send(first, 2)
+    core, to_near = lax.optimization_barrier((core, first))
+    near_first = send(to_near, 1)
     across_first, across_second = send(first, 3), send(second, 3)
 
     def planes(tiles, gots=1):
@@ -353,7 +356,7 @@
     second, low, high = lax.optimization_barrier((second, low, high))
     far_second, near_second = send(second, 2), send(second, 1)
     _, hots, lags = work([far_first, near_first], [], [2, 1], planes((0, 1), 2), low, (0, 1), table, gives_hots=True)
-    _, _, lags = work([far_second, near_second], hots, [], planes((2,), 2), high, (2,), table, lags, BF16)
+    _, _, lags = work([far_second, near_second], hots, [], planes((2,), 2), high, (2,), table, lags, BF16, summed=2 * SUMMED)
     mine = lax.all_to_all(lags.reshape(groups, NB // groups, LAGS), AXES, 0, 0, tiled=True)
     pairs = ROUNDS * block * block * groups // NB
     return summed(mine, 1.0 / (2.0 * math.sqrt(freq_len * width * pairs)))

time: 45.1 us -> 44.6 us (0.989)
  Pallas kernels: 19.4 us -> 18.7 us
    pallas_call x5, Pallas kernels: 16.1 us -> 15.4 us  [stage(): pl.pallas_call(functools.partial(stage_kernel, plan), out_shape=out, in_s...]
where the time goes in v4:
time: 44.6 us; the launch traced here: 44.4 us
  Pallas kernels  18.7 us (42%)
  blocking collectives  14.2 us (32%)
  starting transfers between devices  8.7 us (20%)
  waiting for transfers between devices  1.68 us (4%)
  local copies, waits for them, and re-layouts  1.06 us (2%)
    pallas_call x5, Pallas kernels, stage(): pl.pallas_call(functools.partial(stage_kernel, plan), out_shape=out, in_s...  15.4 us
    all_to_all x1, blocking collectives, on_device(): lax.all_to_all(lags.reshape(groups, NB // groups, LAGS), AXES, 0, 0, tile...  14.2 us
    ppermute x7, starting transfers between devices, swapped(): lax.ppermute(value, AXES, [(source, source ^ mask) for source in range(gr...  8.7 us
    pallas_call x1, Pallas kernels, whiten(): pl.pallas_call(whiten_kernel, out_shape=(sent(firsts + 1), sent(planes -...  2.65 us
    ppermute x7, waiting for transfers between devices, swapped(): lax.ppermute(value, AXES, [(source, source ^ mask) for source in range(gr...  1.68 us
    unnamed x2, local copies, waits for them, and re-layouts  1 us
  transfers between devices with their start and end apart: 7, of which 1 were waited for; matrix products, arithmetic and copies ran while one was open for 0% of the time, Pallas kernels for 30%

profile of v4, /device:TPU:1, one launch (start us, length us, event | category | flops | bytes accessed | tf_op | source)
XLA Modules:
  0.0 44.4 jit_solution(10946531783929870889)
XLA Ops:
  0.0 2.6 %whiten.1 = (bf16[33,32,128]{2,1,0:T(8,128)(2,1)}, bf16[16,32,128]{2,1,0:T(8,128)(2,1)}, bf16[49,32,128]{2,1,0:T(8,128)(2,1)}, bf16[49,32,128]{2,1,0:T(8,128)(2,1)}) custom-call(bf16[32,8,1536]{2,1,0:T(8,128)(2,1)} %spectra_ref.1, s32[4,32,32]{2,1,0:T(8,128)} %bins_ref.1, s32[32]{0:T(128)} %alive_ref.1), custom_call_target="tpu_custom_call" | custom-call | tf_op jit(solution)/shard_map/whiten/pallas_call | solution.py:117
  2.7 0.1 collective-permute-start
  2.8 2.7 %collective-permute-start.1 = (bf16[33,32,128]{2,1,0:T(8,128)(2,1)}, bf16[33,32,128]{2,1,0:T(8,128)(2,1)S(1)}, u32[]{:S(2)}, u32[]{:S(2)}) collective-permute-start(bf16[33,32,128]{2,1,0:T(8,128)(2,1)} %get-tuple-element.38), channel_id=1, source_target_pairs={{0,8},{1,9},{2,10},{3,11},{4,12},{5,13},{6,14},{7,15},{8,0},{9,1},... | collective-permute-start | bytes 811016 | tf_op jit(solution)/shard_map/ppermute | solution.py:42
  5.5 2.3 %collective-permute-start.5 = (bf16[33,32,128]{2,1,0:T(8,128)(2,1)}, bf16[33,32,128]{2,1,0:T(8,128)(2,1)S(1)}, u32[]{:S(2)}, u32[]{:S(2)}) collective-permute-start(bf16[33,32,128]{2,1,0:T(8,128)(2,1)} %get-tuple-element.38), channel_id=1, source_target_pairs={{0,4},{1,5},{2,6},{3,7},{4,0},{5,1},{6,2},{7,3},{8,12},{9,13},{10,... | collective-permute-start | bytes 811016 | tf_op jit(solution)/shard_map/ppermute | solution.py:42
  7.8 0.0 collective-permute-done.refs_1_
  7.8 1.3 %collective-permute-start.6 = (bf16[33,32,128]{2,1,0:T(8,128)(2,1)}, bf16[33,32,128]{2,1,0:T(8,128)(2,1)S(1)}, u32[]{:S(2)}, u32[]{:S(2)}) collective-permute-start(bf16[33,32,128]{2,1,0:T(8,128)(2,1)} %get-tuple-element.38), channel_id=1, source_target_pairs={{0,2},{1,3},{2,0},{3,1},{4,6},{5,7},{6,4},{7,5},{8,10},{9,11},{10,... | collective-permute-start | bytes 811016 | tf_op jit(solution)/shard_map/ppermute | solution.py:42
  9.1 0.3 collective-permute-start.2
  9.3 0.0 copy-start
  9.3 1.0 %copy-done = bf16[49,32,128]{2,1,0:T(8,128)(2,1)S(1)} copy-done((bf16[49,32,128]{2,1,0:T(8,128)(2,1)S(1)}, bf16[49,32,128]{2,1,0:T(8,128)(2,1)}, u32[]{:S(2)}) %copy-start) | copy-done | bytes 401432
  10.3 3.9 %stage.5 = (f32[2,128,128]{2,1,0:T(8,128)S(1)}, f32[2,128,128]{2,1,0:T(8,128)S(1)}, f32[2,128,128]{2,1,0:T(8,128)S(1)}, f32[49,32,128]{2,1,0:T(8,128)S(1)}) custom-call(bf16[49,32,128]{2,1,0:T(8,128)(2,1)S(1)} %copy-done, bf16[49,32,128]{2,1,0:T(8,128)(2,1)S(1)} %collective-permute-done.refs_1_), custom_call_target="tpu_custom_call" | custom-call | tf_op jit(solution)/shard_map/stage/pallas_call | solution.py:290
  14.2 0.0 collective-permute-done.1.refs_1_
  14.2 2.7 %stage.6 = (f32[2,128,128]{2,1,0:T(8,128)S(1)}, f32[2,128,128]{2,1,0:T(8,128)S(1)}, bf16[2,128,1024]{2,1,0:T(8,128)(2,1)S(1)}) custom-call(f32[49,32,128]{2,1,0:T(8,128)S(1)} %get-tuple-element.29.refs_0_, bf16[33,32,128]{2,1,0:T(8,128)(2,1)S(1)} %collective-permute-done.1.refs_1_, f32[2,128,128]{2,1,0:T(8,128)S(1)} %get-tuple-element.31.refs_2_, ...), custom_call_target="tpu_custom_call" | custom-call | tf_op jit(solution)/shard_map/stage/pallas_call | solution.py:290
  16.9 0.0 collective-permute-done.2.refs_1_
  16.9 1.2 %stage.7.refs_5_ = f32[2,128,128]{2,1,0:T(8,128)S(1)} custom-call(f32[49,32,128]{2,1,0:T(8,128)S(1)} %get-tuple-element.29.refs_0_, bf16[16,32,128]{2,1,0:T(8,128)(2,1)S(1)} %collective-permute-done.2.refs_1_, bf16[2,128,1024]{2,1,0:T(8,128)(2,1)S(1)} %get-tuple-element.35.refs_2_, f32[2,128,128]{2,1,0:T(8,128)S(1)} %get-tuple-element.36.refs_3_), custom_call_target="tpu_custom_call" | custom-call | tf_op jit(solution)/shard_map/stage/pallas_call | solution.py:290
  18.1 1.4 %collective-permute-start.3 = (bf16[16,32,128]{2,1,0:T(8,128)(2,1)}, bf16[16,32,128]{2,1,0:T(8,128)(2,1)S(1)}, u32[]{:S(2)}, u32[]{:S(2)}) collective-permute-start(bf16[16,32,128]{2,1,0:T(8,128)(2,1)} %get-tuple-element.37), channel_id=1, source_target_pairs={{0,4},{1,5},{2,6},{3,7},{4,0},{5,1},{6,2},{7,3},{8,12},{9,13},{10,... | collective-permute-start | bytes 393224 | tf_op jit(solution)/shard_map/ppermute | solution.py:42
  19.5 0.7 %collective-permute-start.4 = (bf16[16,32,128]{2,1,0:T(8,128)(2,1)}, bf16[16,32,128]{2,1,0:T(8,128)(2,1)S(1)}, u32[]{:S(2)}, u32[]{:S(2)}) collective-permute-start(bf16[16,32,128]{2,1,0:T(8,128)(2,1)} %get-tuple-element.37), channel_id=1, source_target_pairs={{0,2},{1,3},{2,0},{3,1},{4,6},{5,7},{6,4},{7,5},{8,10},{9,11},{10,... | collective-permute-start | bytes 393224 | tf_op jit(solution)/shard_map/ppermute | solution.py:42
  20.2 0.0 collective-permute-done.5.refs_1_
  20.2 0.0 collective-permute-done.6.refs_2_
  20.2 5.4 %stage.8 = (f32[128,896]{1,0:T(8,128)S(1)}, bf16[2,128,1024]{2,1,0:T(8,128)(2,1)S(1)}, bf16[2,128,1024]{2,1,0:T(8,128)(2,1)S(1)}) custom-call(f32[49,32,128]{2,1,0:T(8,128)S(1)} %get-tuple-element.29.refs_0_, bf16[33,32,128]{2,1,0:T(8,128)(2,1)S(1)} %collective-permute-done.5.refs_1_, bf16[33,32,128]{2,1,0:T(8,128)(2,1)S(1)} %collective-permute-done.6.refs_2_, ...), custom_call_target="tpu_custom_call" | custom-call | tf_op jit(solution)/shard_map/stage/pallas_call | solution.py:290
  25.6 1.7 %collective-permute-done.3.refs_1_ = bf16[16,32,128]{2,1,0:T(8,128)(2,1)S(1)} collective-permute-done((bf16[16,32,128]{2,1,0:T(8,128)(2,1)}, bf16[16,32,128]{2,1,0:T(8,128)(2,1)S(1)}, u32[]{:S(2)}, u32[]{:S(2)}) %collective-permute-start.3) | collective-permute-done | bytes 131104 | tf_op jit(solution)/shard_map/ppermute | solution.py:42
  27.3 0.0 collective-permute-done.4.refs_2_
  27.3 2.2 %stage.9 = bf16[128,896]{1,0:T(8,128)(2,1)S(1)} custom-call(f32[49,32,128]{2,1,0:T(8,128)S(1)} %get-tuple-element.29.refs_0_, bf16[16,32,128]{2,1,0:T(8,128)(2,1)S(1)} %collective-permute-done.3.refs_1_, bf16[16,32,128]{2,1,0:T(8,128)(2,1)S(1)} %collective-permute-done.4.refs_2_, bf16[2,128,1024]{2,1,0:T(8,128)(2,1)S(1)} %get-tuple-element.41.refs_3_, ...), custom_call_target="tpu_custom_call" | custom-call | tf_op jit(solution)/shard_map/stage/pallas_call | solution.py:290
  29.5 0.1 reshape.3
  29.6 14.2 %all_to_all.5.parts_ref = bf16[32,4,896]{2,1,0:T(4,128)(2,1)S(1)} all-to-all(bf16[32,4,896]{2,1,0:T(4,128)(2,1)S(1)} %reshape.3), channel_id=1, replica_groups=mesh['row'=4,'col'=8] {'row','col'}, dimensions={0} | all-to-all | bytes 458752 | tf_op jit(solution)/shard_map/all_to_all | solution.py:360
  43.8 0.7 %summed.1 = f32[4,896]{1,0:T(4,128)} custom-call(bf16[32,4,896]{2,1,0:T(4,128)(2,1)S(1)} %all_to_all.5.parts_ref), custom_call_target="tpu_custom_call" | custom-call | tf_op jit(solution)/shard_map/summed/pallas_call | solution.py:312
Async XLA Ops:
  2.7 5.1 %collective-permute-start = (bf16[49,32,128]{2,1,0:T(8,128)(2,1)}, bf16[49,32,128]{2,1,0:T(8,128)(2,1)S(1)}, u32[]{:S(2)}, u32[]{:S(2)}) collective-permute-start(bf16[49,32,128]{2,1,0:T(8,128)(2,1)} %get-tuple-element.26), channel_id=1, source_target_pairs={{0,1},{1,0},{2,3},{3,2},{4,5},{5,4},{6,7},{7,6},{8,9},{9,8},{10,11... | collective-permute-start | bytes 1204232 | tf_op jit(solution)/shard_map/ppermute | solution.py:42
  2.8 11.4 %collective-permute-start.1 = (bf16[33,32,128]{2,1,0:T(8,128)(2,1)}, bf16[33,32,128]{2,1,0:T(8,128)(2,1)S(1)}, u32[]{:S(2)}, u32[]{:S(2)}) collective-permute-start(bf16[33,32,128]{2,1,0:T(8,128)(2,1)} %get-tuple-element.38), channel_id=1, source_target_pairs={{0,8},{1,9},{2,10},{3,11},{4,12},{5,13},{6,14},{7,15},{8,0},{9,1},... | collective-permute-start | bytes 811016 | tf_op jit(solution)/shard_map/ppermute | solution.py:42
  5.5 14.7 %collective-permute-start.5 = (bf16[33,32,128]{2,1,0:T(8,128)(2,1)}, bf16[33,32,128]{2,1,0:T(8,128)(2,1)S(1)}, u32[]{:S(2)}, u32[]{:S(2)}) collective-permute-start(bf16[33,32,128]{2,1,0:T(8,128)(2,1)} %get-tuple-element.38), channel_id=1, source_target_pairs={{0,4},{1,5},{2,6},{3,7},{4,0},{5,1},{6,2},{7,3},{8,12},{9,13},{10,... | collective-permute-start | bytes 811016 | tf_op jit(solution)/shard_map/ppermute | solution.py:42
  7.8 12.4 %collective-permute-start.6 = (bf16[33,32,128]{2,1,0:T(8,128)(2,1)}, bf16[33,32,128]{2,1,0:T(8,128)(2,1)S(1)}, u32[]{:S(2)}, u32[]{:S(2)}) collective-permute-start(bf16[33,32,128]{2,1,0:T(8,128)(2,1)} %get-tuple-element.38), channel_id=1, source_target_pairs={{0,2},{1,3},{2,0},{3,1},{4,6},{5,7},{6,4},{7,5},{8,10},{9,11},{10,... | collective-permute-start | bytes 811016 | tf_op jit(solution)/shard_map/ppermute | solution.py:42
  9.1 7.9 %collective-permute-start.2 = (bf16[16,32,128]{2,1,0:T(8,128)(2,1)}, bf16[16,32,128]{2,1,0:T(8,128)(2,1)S(1)}, u32[]{:S(2)}, u32[]{:S(2)}) collective-permute-start(bf16[16,32,128]{2,1,0:T(8,128)(2,1)} %get-tuple-element.37), channel_id=1, source_target_pairs={{0,8},{1,9},{2,10},{3,11},{4,12},{5,13},{6,14},{7,15},{8,0},{9,1},... | collective-permute-start | bytes 393224 | tf_op jit(solution)/shard_map/ppermute | solution.py:42
  9.3 1.0 %copy-start = (bf16[49,32,128]{2,1,0:T(8,128)(2,1)S(1)}, bf16[49,32,128]{2,1,0:T(8,128)(2,1)}, u32[]{:S(2)}) copy-start(bf16[49,32,128]{2,1,0:T(8,128)(2,1)} %get-tuple-element.25.refs_0_) | copy-start | bytes 1204228
  18.1 9.1 %collective-permute-start.3 = (bf16[16,32,128]{2,1,0:T(8,128)(2,1)}, bf16[16,32,128]{2,1,0:T(8,128)(2,1)S(1)}, u32[]{:S(2)}, u32[]{:S(2)}) collective-permute-start(bf16[16,32,128]{2,1,0:T(8,128)(2,1)} %get-tuple-element.37), channel_id=1, source_target_pairs={{0,4},{1,5},{2,6},{3,7},{4,0},{5,1},{6,2},{7,3},{8,12},{9,13},{10,... | collective-permute-start | bytes 393224 | tf_op jit(solution)/shard_map/ppermute | solution.py:42
  19.5 7.8 %collective-permute-start.4 = (bf16[16,32,128]{2,1,0:T(8,128)(2,1)}, bf16[16,32,128]{2,1,0:T(8,128)(2,1)S(1)}, u32[]{:S(2)}, u32[]{:S(2)}) collective-permute-start(bf16[16,32,128]{2,1,0:T(8,128)(2,1)} %get-tuple-element.37), channel_id=1, source_target_pairs={{0,2},{1,3},{2,0},{3,1},{4,6},{5,7},{6,4},{7,5},{8,10},{9,11},{10,... | collective-permute-start | bytes 393224 | tf_op jit(solution)/shard_map/ppermute | solution.py:42

commit v5 on v4

--- a/solution.py
+++ b/solution.py
@@ -64,9 +64,18 @@
     ]
     bins_copy = pltpu.make_async_copy(bins_ref, loaded_bins_ref, sems.at[block // STEP])
     alive_copy = pltpu.make_async_copy(alive_ref, loaded_alive_ref, sems.at[block // STEP + 1])
-    for copy in [*copies, alive_copy, bins_copy]:
+    for copy in [bins_copy, alive_copy, *copies]:
         copy.start()
     half = half_here()
+    planes = sent_ref.shape[0] - 1
+    firsts = first_ref.shape[0] - 1
+    bins_copy.wait()
+    bins = jnp.zeros((block, LANES), F32)
+    for round_no in range(bins_ref.shape[0]):
+        place = one_hot(block, LANES, -block * round_no, lambda ids: ids)
+        bins = bins + jnp.dot(loaded_bins_ref[round_no].astype(F32).astype(BF16), place, preferred_element_type=F32)
+    sent_ref[planes] = bins.astype(BF16)
+    kept_ref[planes] = bins.astype(BF16)
     for channel in range(block):
         if channel % STEP == 0:
             copies[channel // STEP].wait()
@@ -77,21 +86,12 @@
         values = values * (lax.rsqrt(powers + 1e-06) * loaded_alive_ref[channel].astype(F32))
         for tile in range(columns // LANES):
             scaled_ref[tile, channel * width : (channel + 1) * width, :] = values[:, tile * LANES : (tile + 1) * LANES]
-    planes = sent_ref.shape[0] - 1
-    firsts = first_ref.shape[0] - 1
     going = []
 
     def go(source, target):
         going.append(pltpu.make_async_copy(source, target, out_sems.at[len(going)]))
         going[-1].start()
 
-    bins_copy.wait()
-    bins = jnp.zeros((block, LANES), F32)
-    for round_no in range(bins_ref.shape[0]):
-        place = one_hot(block, LANES, -block * round_no, lambda ids: ids)
-        bins = bins + jnp.dot(loaded_bins_ref[round_no].astype(F32).astype(BF16), place, preferred_element_type=F32)
-    sent_ref[planes] = bins.astype(BF16)
-    kept_ref[planes] = bins.astype(BF16)
     for plane in range(planes):
         sent_ref[plane] = plane_of(scaled_ref, plane, block, 1 - half).astype(BF16)
         if plane == firsts - 1:
@@ -154,29 +154,29 @@
     block = keep_ref.shape[1]
 
     def of_channel(channel, carry):
-        ones = [
-            jnp.broadcast_to(keep_ref[here + k, pl.ds(channel, 1), :], (ROWS, LANES)).astype(BF16)
-            for k in range(2 * width)
-        ]
-        for number, (got_ref, there) in enumerate(gots):
-            for start in range(0, block, ROWS):
-                at = pl.ds(pl.multiple_of(channel * block + start, ROWS), ROWS)
-                for some in range(width // summed):
-                    real, imag = None, None
-                    for window in range(some * summed, (some + 1) * summed):
-                        one_real, one_imag = ones[2 * window], ones[2 * window + 1]
+        for some in range(width // summed):
+            sums = {}
+            for window in range(some * summed, (some + 1) * summed):
+                one_real, one_imag = [
+                    jnp.broadcast_to(keep_ref[here + 2 * window + k, pl.ds(channel, 1), :], (ROWS, LANES)).astype(BF16)
+                    for k in range(2)
+                ]
+                for number, (got_ref, there) in enumerate(gots):
+                    for start in range(0, block, ROWS):
                         two_real = got_ref[there + 2 * window, start : start + ROWS, :]
                         two_imag = got_ref[there + 2 * window + 1, start : start + ROWS, :]
-                        more_real = one_real * two_real + one_imag * two_imag
-                        more_imag = one_imag * two_real - one_real * two_imag
-                        real = more_real if real is None else real + more_real
-                        imag = more_imag if imag is None else imag + more_imag
-                    lanes = slice(some % 2 * LANES, (some % 2 + 1) * LANES)
-                    cross_ref[number, 0, some // 2, at, lanes] = real
-                    cross_ref[number, 1, some // 2, at, lanes] = imag
+                        real = one_real * two_real + one_imag * two_imag
+                        imag = one_imag * two_real - one_real * two_imag
+                        old = sums.get((number, start))
+                        sums[number, start] = (real, imag) if old is None else (old[0] + real, old[1] + imag)
+            lanes = slice(some % 2 * LANES, (some % 2 + 1) * LANES)
+            for (number, start), pair in sums.items():
+                at = pl.ds(pl.multiple_of(channel * block + start, ROWS), ROWS)
+                for part in range(2):
+                    cross_ref[number, part, some // 2, at, lanes] = pair[part]
         return carry
 
-    lax.fori_loop(0, block, of_channel, 0, unroll=16 // len(gots))
+    lax.fori_loop(0, block, of_channel, 0, unroll=8 // len(gots))
 
 
 def binned(hots_refs, cross_ref, part):

time: 44.6 us -> 44.7 us (level)
  no operation moved by 1% of the time
where the time goes in v5:
time: 44.7 us; the launch traced here: 44.5 us
  Pallas kernels  18.8 us (42%)
  blocking collectives  14.3 us (32%)
  starting transfers between devices  8.64 us (19%)
  waiting for transfers between devices  1.62 us (4%)
  local copies, waits for them, and re-layouts  1.06 us (2%)
    pallas_call x5, Pallas kernels, stage(): pl.pallas_call(functools.partial(stage_kernel, plan), out_shape=out, in_s...  15.5 us
    all_to_all x1, blocking collectives, on_device(): lax.all_to_all(lags.reshape(groups, NB // groups, LAGS), AXES, 0, 0, tile...  14.3 us
    ppermute x7, starting transfers between devices, swapped(): lax.ppermute(value, AXES, [(source, source ^ mask) for source in range(gr...  8.64 us
    pallas_call x1, Pallas kernels, whiten(): pl.pallas_call(whiten_kernel, out_shape=(sent(firsts + 1), sent(planes -...  2.65 us
    ppermute x7, waiting for transfers between devices, swapped(): lax.ppermute(value, AXES, [(source, source ^ mask) for source in range(gr...  1.62 us
    unnamed x2, local copies, waits for them, and re-layouts  1 us
  transfers between devices with their start and end apart: 7, of which 1 were waited for; matrix products, arithmetic and copies ran while one was open for 0% of the time, Pallas kernels for 30%

profile of v5, /device:TPU:1, one launch (start us, length us, event | category | flops | bytes accessed | tf_op | source)
XLA Modules:
  0.0 44.5 jit_solution(13857634859050129541)
XLA Ops:
  0.0 2.7 %whiten.1 = (bf16[33,32,128]{2,1,0:T(8,128)(2,1)}, bf16[16,32,128]{2,1,0:T(8,128)(2,1)}, bf16[49,32,128]{2,1,0:T(8,128)(2,1)}, bf16[49,32,128]{2,1,0:T(8,128)(2,1)}) custom-call(bf16[32,8,1536]{2,1,0:T(8,128)(2,1)} %spectra_ref.1, s32[4,32,32]{2,1,0:T(8,128)} %bins_ref.1, s32[32]{0:T(128)} %alive_ref.1), custom_call_target="tpu_custom_call" | custom-call | tf_op jit(solution)/shard_map/whiten/pallas_call | solution.py:117
  2.7 0.1 collective-permute-start
  2.8 2.7 %collective-permute-start.1 = (bf16[33,32,128]{2,1,0:T(8,128)(2,1)}, bf16[33,32,128]{2,1,0:T(8,128)(2,1)S(1)}, u32[]{:S(2)}, u32[]{:S(2)}) collective-permute-start(bf16[33,32,128]{2,1,0:T(8,128)(2,1)} %get-tuple-element.38), channel_id=1, source_target_pairs={{0,8},{1,9},{2,10},{3,11},{4,12},{5,13},{6,14},{7,15},{8,0},{9,1},... | collective-permute-start | bytes 811016 | tf_op jit(solution)/shard_map/ppermute | solution.py:42
  5.5 2.3 %collective-permute-start.5 = (bf16[33,32,128]{2,1,0:T(8,128)(2,1)}, bf16[33,32,128]{2,1,0:T(8,128)(2,1)S(1)}, u32[]{:S(2)}, u32[]{:S(2)}) collective-permute-start(bf16[33,32,128]{2,1,0:T(8,128)(2,1)} %get-tuple-element.38), channel_id=1, source_target_pairs={{0,4},{1,5},{2,6},{3,7},{4,0},{5,1},{6,2},{7,3},{8,12},{9,13},{10,... | collective-permute-start | bytes 811016 | tf_op jit(solution)/shard_map/ppermute | solution.py:42
  7.8 0.0 collective-permute-done.refs_1_
  7.8 1.3 %collective-permute-start.6 = (bf16[33,32,128]{2,1,0:T(8,128)(2,1)}, bf16[33,32,128]{2,1,0:T(8,128)(2,1)S(1)}, u32[]{:S(2)}, u32[]{:S(2)}) collective-permute-start(bf16[33,32,128]{2,1,0:T(8,128)(2,1)} %get-tuple-element.38), channel_id=1, source_target_pairs={{0,2},{1,3},{2,0},{3,1},{4,6},{5,7},{6,4},{7,5},{8,10},{9,11},{10,... | collective-permute-start | bytes 811016 | tf_op jit(solution)/shard_map/ppermute | solution.py:42
  9.1 0.3 collective-permute-start.2
  9.3 0.0 copy-start
  9.3 1.0 %copy-done = bf16[49,32,128]{2,1,0:T(8,128)(2,1)S(1)} copy-done((bf16[49,32,128]{2,1,0:T(8,128)(2,1)S(1)}, bf16[49,32,128]{2,1,0:T(8,128)(2,1)}, u32[]{:S(2)}) %copy-start) | copy-done | bytes 401432
  10.3 3.9 %stage.5 = (f32[2,128,128]{2,1,0:T(8,128)S(1)}, f32[2,128,128]{2,1,0:T(8,128)S(1)}, f32[2,128,128]{2,1,0:T(8,128)S(1)}, f32[49,32,128]{2,1,0:T(8,128)S(1)}) custom-call(bf16[49,32,128]{2,1,0:T(8,128)(2,1)S(1)} %copy-done, bf16[49,32,128]{2,1,0:T(8,128)(2,1)S(1)} %collective-permute-done.refs_1_), custom_call_target="tpu_custom_call" | custom-call | tf_op jit(solution)/shard_map/stage/pallas_call | solution.py:290
  14.3 0.0 collective-permute-done.1.refs_1_
  14.3 2.7 %stage.6 = (f32[2,128,128]{2,1,0:T(8,128)S(1)}, f32[2,128,128]{2,1,0:T(8,128)S(1)}, bf16[2,128,1024]{2,1,0:T(8,128)(2,1)S(1)}) custom-call(f32[49,32,128]{2,1,0:T(8,128)S(1)} %get-tuple-element.29.refs_0_, bf16[33,32,128]{2,1,0:T(8,128)(2,1)S(1)} %collective-permute-done.1.refs_1_, f32[2,128,128]{2,1,0:T(8,128)S(1)} %get-tuple-element.31.refs_2_, ...), custom_call_target="tpu_custom_call" | custom-call | tf_op jit(solution)/shard_map/stage/pallas_call | solution.py:290
  17.0 0.0 collective-permute-done.2.refs_1_
  17.0 1.2 %stage.7.refs_5_ = f32[2,128,128]{2,1,0:T(8,128)S(1)} custom-call(f32[49,32,128]{2,1,0:T(8,128)S(1)} %get-tuple-element.29.refs_0_, bf16[16,32,128]{2,1,0:T(8,128)(2,1)S(1)} %collective-permute-done.2.refs_1_, bf16[2,128,1024]{2,1,0:T(8,128)(2,1)S(1)} %get-tuple-element.35.refs_2_, f32[2,128,128]{2,1,0:T(8,128)S(1)} %get-tuple-element.36.refs_3_), custom_call_target="tpu_custom_call" | custom-call | tf_op jit(solution)/shard_map/stage/pallas_call | solution.py:290
  18.2 1.4 %collective-permute-start.3 = (bf16[16,32,128]{2,1,0:T(8,128)(2,1)}, bf16[16,32,128]{2,1,0:T(8,128)(2,1)S(1)}, u32[]{:S(2)}, u32[]{:S(2)}) collective-permute-start(bf16[16,32,128]{2,1,0:T(8,128)(2,1)} %get-tuple-element.37), channel_id=1, source_target_pairs={{0,4},{1,5},{2,6},{3,7},{4,0},{5,1},{6,2},{7,3},{8,12},{9,13},{10,... | collective-permute-start | bytes 393224 | tf_op jit(solution)/shard_map/ppermute | solution.py:42
  19.6 0.6 %collective-permute-start.4 = (bf16[16,32,128]{2,1,0:T(8,128)(2,1)}, bf16[16,32,128]{2,1,0:T(8,128)(2,1)S(1)}, u32[]{:S(2)}, u32[]{:S(2)}) collective-permute-start(bf16[16,32,128]{2,1,0:T(8,128)(2,1)} %get-tuple-element.37), channel_id=1, source_target_pairs={{0,2},{1,3},{2,0},{3,1},{4,6},{5,7},{6,4},{7,5},{8,10},{9,11},{10,... | collective-permute-start | bytes 393224 | tf_op jit(solution)/shard_map/ppermute | solution.py:42
  20.2 0.0 collective-permute-done.5.refs_1_
  20.2 0.0 collective-permute-done.6.refs_2_
  20.2 5.5 %stage.8 = (f32[128,896]{1,0:T(8,128)S(1)}, bf16[2,128,1024]{2,1,0:T(8,128)(2,1)S(1)}, bf16[2,128,1024]{2,1,0:T(8,128)(2,1)S(1)}) custom-call(f32[49,32,128]{2,1,0:T(8,128)S(1)} %get-tuple-element.29.refs_0_, bf16[33,32,128]{2,1,0:T(8,128)(2,1)S(1)} %collective-permute-done.5.refs_1_, bf16[33,32,128]{2,1,0:T(8,128)(2,1)S(1)} %collective-permute-done.6.refs_2_, ...), custom_call_target="tpu_custom_call" | custom-call | tf_op jit(solution)/shard_map/stage/pallas_call | solution.py:290
  25.7 1.6 %collective-permute-done.3.refs_1_ = bf16[16,32,128]{2,1,0:T(8,128)(2,1)S(1)} collective-permute-done((bf16[16,32,128]{2,1,0:T(8,128)(2,1)}, bf16[16,32,128]{2,1,0:T(8,128)(2,1)S(1)}, u32[]{:S(2)}, u32[]{:S(2)}) %collective-permute-start.3) | collective-permute-done | bytes 131104 | tf_op jit(solution)/shard_map/ppermute | solution.py:42
  27.3 0.0 collective-permute-done.4.refs_2_
  27.3 2.2 %stage.9 = bf16[128,896]{1,0:T(8,128)(2,1)S(1)} custom-call(f32[49,32,128]{2,1,0:T(8,128)S(1)} %get-tuple-element.29.refs_0_, bf16[16,32,128]{2,1,0:T(8,128)(2,1)S(1)} %collective-permute-done.3.refs_1_, bf16[16,32,128]{2,1,0:T(8,128)(2,1)S(1)} %collective-permute-done.4.refs_2_, bf16[2,128,1024]{2,1,0:T(8,128)(2,1)S(1)} %get-tuple-element.41.refs_3_, ...), custom_call_target="tpu_custom_call" | custom-call | tf_op jit(solution)/shard_map/stage/pallas_call | solution.py:290
  29.5 0.1 reshape.3
  29.6 14.3 %all_to_all.5.parts_ref = bf16[32,4,896]{2,1,0:T(4,128)(2,1)S(1)} all-to-all(bf16[32,4,896]{2,1,0:T(4,128)(2,1)S(1)} %reshape.3), channel_id=1, replica_groups=mesh['row'=4,'col'=8] {'row','col'}, dimensions={0} | all-to-all | bytes 458752 | tf_op jit(solution)/shard_map/all_to_all | solution.py:360
  43.8 0.7 %summed.1 = f32[4,896]{1,0:T(4,128)} custom-call(bf16[32,4,896]{2,1,0:T(4,128)(2,1)S(1)} %all_to_all.5.parts_ref), custom_call_target="tpu_custom_call" | custom-call | tf_op jit(solution)/shard_map/summed/pallas_call | solution.py:312
Async XLA Ops:
  2.7 5.1 %collective-permute-start = (bf16[49,32,128]{2,1,0:T(8,128)(2,1)}, bf16[49,32,128]{2,1,0:T(8,128)(2,1)S(1)}, u32[]{:S(2)}, u32[]{:S(2)}) collective-permute-start(bf16[49,32,128]{2,1,0:T(8,128)(2,1)} %get-tuple-element.26), channel_id=1, source_target_pairs={{0,1},{1,0},{2,3},{3,2},{4,5},{5,4},{6,7},{7,6},{8,9},{9,8},{10,11... | collective-permute-start | bytes 1204232 | tf_op jit(solution)/shard_map/ppermute | solution.py:42
  2.8 11.5 %collective-permute-start.1 = (bf16[33,32,128]{2,1,0:T(8,128)(2,1)}, bf16[33,32,128]{2,1,0:T(8,128)(2,1)S(1)}, u32[]{:S(2)}, u32[]{:S(2)}) collective-permute-start(bf16[33,32,128]{2,1,0:T(8,128)(2,1)} %get-tuple-element.38), channel_id=1, source_target_pairs={{0,8},{1,9},{2,10},{3,11},{4,12},{5,13},{6,14},{7,15},{8,0},{9,1},... | collective-permute-start | bytes 811016 | tf_op jit(solution)/shard_map/ppermute | solution.py:42
  5.5 14.7 %collective-permute-start.5 = (bf16[33,32,128]{2,1,0:T(8,128)(2,1)}, bf16[33,32,128]{2,1,0:T(8,128)(2,1)S(1)}, u32[]{:S(2)}, u32[]{:S(2)}) collective-permute-start(bf16[33,32,128]{2,1,0:T(8,128)(2,1)} %get-tuple-element.38), channel_id=1, source_target_pairs={{0,4},{1,5},{2,6},{3,7},{4,0},{5,1},{6,2},{7,3},{8,12},{9,13},{10,... | collective-permute-start | bytes 811016 | tf_op jit(solution)/shard_map/ppermute | solution.py:42
  7.8 12.4 %collective-permute-start.6 = (bf16[33,32,128]{2,1,0:T(8,128)(2,1)}, bf16[33,32,128]{2,1,0:T(8,128)(2,1)S(1)}, u32[]{:S(2)}, u32[]{:S(2)}) collective-permute-start(bf16[33,32,128]{2,1,0:T(8,128)(2,1)} %get-tuple-element.38), channel_id=1, source_target_pairs={{0,2},{1,3},{2,0},{3,1},{4,6},{5,7},{6,4},{7,5},{8,10},{9,11},{10,... | collective-permute-start | bytes 811016 | tf_op jit(solution)/shard_map/ppermute | solution.py:42
  9.1 7.9 %collective-permute-start.2 = (bf16[16,32,128]{2,1,0:T(8,128)(2,1)}, bf16[16,32,128]{2,1,0:T(8,128)(2,1)S(1)}, u32[]{:S(2)}, u32[]{:S(2)}) collective-permute-start(bf16[16,32,128]{2,1,0:T(8,128)(2,1)} %get-tuple-element.37), channel_id=1, source_target_pairs={{0,8},{1,9},{2,10},{3,11},{4,12},{5,13},{6,14},{7,15},{8,0},{9,1},... | collective-permute-start | bytes 393224 | tf_op jit(solution)/shard_map/ppermute | solution.py:42
  9.3 1.0 %copy-start = (bf16[49,32,128]{2,1,0:T(8,128)(2,1)S(1)}, bf16[49,32,128]{2,1,0:T(8,128)(2,1)}, u32[]{:S(2)}) copy-start(bf16[49,32,128]{2,1,0:T(8,128)(2,1)} %get-tuple-element.25.refs_0_) | copy-start | bytes 1204228
  18.2 9.1 %collective-permute-start.3 = (bf16[16,32,128]{2,1,0:T(8,128)(2,1)}, bf16[16,32,128]{2,1,0:T(8,128)(2,1)S(1)}, u32[]{:S(2)}, u32[]{:S(2)}) collective-permute-start(bf16[16,32,128]{2,1,0:T(8,128)(2,1)} %get-tuple-element.37), channel_id=1, source_target_pairs={{0,4},{1,5},{2,6},{3,7},{4,0},{5,1},{6,2},{7,3},{8,12},{9,13},{10,... | collective-permute-start | bytes 393224 | tf_op jit(solution)/shard_map/ppermute | solution.py:42
  19.6 7.7 %collective-permute-start.4 = (bf16[16,32,128]{2,1,0:T(8,128)(2,1)}, bf16[16,32,128]{2,1,0:T(8,128)(2,1)S(1)}, u32[]{:S(2)}, u32[]{:S(2)}) collective-permute-start(bf16[16,32,128]{2,1,0:T(8,128)(2,1)} %get-tuple-element.37), channel_id=1, source_target_pairs={{0,2},{1,3},{2,0},{3,1},{4,6},{5,7},{6,4},{7,5},{8,10},{9,11},{10,... | collective-permute-start | bytes 393224 | tf_op jit(solution)/shard_map/ppermute | solution.py:42

commit v6 on v5

--- a/solution.py
+++ b/solution.py
@@ -201,9 +201,8 @@
     values = jnp.concatenate(sums, axis=1)
     high = values.astype(BF16)
     low = (values - high.astype(F32)).astype(BF16)
-    result = jnp.dot(high, loaded_ref[0], preferred_element_type=F32)
-    result = result + jnp.dot(low, loaded_ref[0], preferred_element_type=F32)
-    return result + jnp.dot(high, loaded_ref[1], preferred_element_type=F32)
+    both = jnp.dot(jnp.concatenate([high, low], axis=0), loaded_ref[0], preferred_element_type=F32)
+    return both[:NB] + both[NB:] + jnp.dot(high, loaded_ref[1], preferred_element_type=F32)
 
 
 def stage_kernel(plan, *refs):

time: 44.7 us -> 44.7 us (level)
  no operation moved by 1% of the time
where the time goes in v6:
time: 44.7 us; the launch traced here: 44.5 us
  Pallas kernels  18.8 us (42%)
  blocking collectives  14.3 us (32%)
  starting transfers between devices  8.64 us (19%)
  waiting for transfers between devices  1.63 us (4%)
  local copies, waits for them, and re-layouts  1.06 us (2%)
    pallas_call x5, Pallas kernels, stage(): pl.pallas_call(functools.partial(stage_kernel, plan), out_shape=out, in_s...  15.5 us
    all_to_all x1, blocking collectives, on_device(): lax.all_to_all(lags.reshape(groups, NB // groups, LAGS), AXES, 0, 0, tile...  14.3 us
    ppermute x7, starting transfers between devices, swapped(): lax.ppermute(value, AXES, [(source, source ^ mask) for source in range(gr...  8.64 us
    pallas_call x1, Pallas kernels, whiten(): pl.pallas_call(whiten_kernel, out_shape=(sent(firsts + 1), sent(planes -...  2.65 us
    ppermute x7, waiting for transfers between devices, swapped(): lax.ppermute(value, AXES, [(source, source ^ mask) for source in range(gr...  1.63 us
    unnamed x2, local copies, waits for them, and re-layouts  1 us
  transfers between devices with their start and end apart: 7, of which 1 were waited for; matrix products, arithmetic and copies ran while one was open for 0% of the time, Pallas kernels for 30%

profile of v6, /device:TPU:1, one launch (start us, length us, event | category | flops | bytes accessed | tf_op | source)
XLA Modules:
  0.0 44.5 jit_solution(15121297575834947094)
XLA Ops:
  0.0 2.7 %whiten.1 = (bf16[33,32,128]{2,1,0:T(8,128)(2,1)}, bf16[16,32,128]{2,1,0:T(8,128)(2,1)}, bf16[49,32,128]{2,1,0:T(8,128)(2,1)}, bf16[49,32,128]{2,1,0:T(8,128)(2,1)}) custom-call(bf16[32,8,1536]{2,1,0:T(8,128)(2,1)} %spectra_ref.1, s32[4,32,32]{2,1,0:T(8,128)} %bins_ref.1, s32[32]{0:T(128)} %alive_ref.1), custom_call_target="tpu_custom_call" | custom-call | tf_op jit(solution)/shard_map/whiten/pallas_call | solution.py:117
  2.7 0.1 collective-permute-start
  2.8 2.7 %collective-permute-start.1 = (bf16[33,32,128]{2,1,0:T(8,128)(2,1)}, bf16[33,32,128]{2,1,0:T(8,128)(2,1)S(1)}, u32[]{:S(2)}, u32[]{:S(2)}) collective-permute-start(bf16[33,32,128]{2,1,0:T(8,128)(2,1)} %get-tuple-element.38), channel_id=1, source_target_pairs={{0,8},{1,9},{2,10},{3,11},{4,12},{5,13},{6,14},{7,15},{8,0},{9,1},... | collective-permute-start | bytes 811016 | tf_op jit(solution)/shard_map/ppermute | solution.py:42
  5.5 2.3 %collective-permute-start.5 = (bf16[33,32,128]{2,1,0:T(8,128)(2,1)}, bf16[33,32,128]{2,1,0:T(8,128)(2,1)S(1)}, u32[]{:S(2)}, u32[]{:S(2)}) collective-permute-start(bf16[33,32,128]{2,1,0:T(8,128)(2,1)} %get-tuple-element.38), channel_id=1, source_target_pairs={{0,4},{1,5},{2,6},{3,7},{4,0},{5,1},{6,2},{7,3},{8,12},{9,13},{10,... | collective-permute-start | bytes 811016 | tf_op jit(solution)/shard_map/ppermute | solution.py:42
  7.8 0.0 collective-permute-done.refs_1_
  7.8 1.3 %collective-permute-start.6 = (bf16[33,32,128]{2,1,0:T(8,128)(2,1)}, bf16[33,32,128]{2,1,0:T(8,128)(2,1)S(1)}, u32[]{:S(2)}, u32[]{:S(2)}) collective-permute-start(bf16[33,32,128]{2,1,0:T(8,128)(2,1)} %get-tuple-element.38), channel_id=1, source_target_pairs={{0,2},{1,3},{2,0},{3,1},{4,6},{5,7},{6,4},{7,5},{8,10},{9,11},{10,... | collective-permute-start | bytes 811016 | tf_op jit(solution)/shard_map/ppermute | solution.py:42
  9.1 0.3 collective-permute-start.2
  9.3 0.0 copy-start
  9.3 1.0 %copy-done = bf16[49,32,128]{2,1,0:T(8,128)(2,1)S(1)} copy-done((bf16[49,32,128]{2,1,0:T(8,128)(2,1)S(1)}, bf16[49,32,128]{2,1,0:T(8,128)(2,1)}, u32[]{:S(2)}) %copy-start) | copy-done | bytes 401432
  10.3 3.9 %stage.5 = (f32[2,128,128]{2,1,0:T(8,128)S(1)}, f32[2,128,128]{2,1,0:T(8,128)S(1)}, f32[2,128,128]{2,1,0:T(8,128)S(1)}, f32[49,32,128]{2,1,0:T(8,128)S(1)}) custom-call(bf16[49,32,128]{2,1,0:T(8,128)(2,1)S(1)} %copy-done, bf16[49,32,128]{2,1,0:T(8,128)(2,1)S(1)} %collective-permute-done.refs_1_), custom_call_target="tpu_custom_call" | custom-call | tf_op jit(solution)/shard_map/stage/pallas_call | solution.py:289
  14.3 0.0 collective-permute-done.1.refs_1_
  14.3 2.7 %stage.6 = (f32[2,128,128]{2,1,0:T(8,128)S(1)}, f32[2,128,128]{2,1,0:T(8,128)S(1)}, bf16[2,128,1024]{2,1,0:T(8,128)(2,1)S(1)}) custom-call(f32[49,32,128]{2,1,0:T(8,128)S(1)} %get-tuple-element.29.refs_0_, bf16[33,32,128]{2,1,0:T(8,128)(2,1)S(1)} %collective-permute-done.1.refs_1_, f32[2,128,128]{2,1,0:T(8,128)S(1)} %get-tuple-element.31.refs_2_, ...), custom_call_target="tpu_custom_call" | custom-call | tf_op jit(solution)/shard_map/stage/pallas_call | solution.py:289
  17.0 0.0 collective-permute-done.2.refs_1_
  17.0 1.2 %stage.7.refs_5_ = f32[2,128,128]{2,1,0:T(8,128)S(1)} custom-call(f32[49,32,128]{2,1,0:T(8,128)S(1)} %get-tuple-element.29.refs_0_, bf16[16,32,128]{2,1,0:T(8,128)(2,1)S(1)} %collective-permute-done.2.refs_1_, bf16[2,128,1024]{2,1,0:T(8,128)(2,1)S(1)} %get-tuple-element.35.refs_2_, f32[2,128,128]{2,1,0:T(8,128)S(1)} %get-tuple-element.36.refs_3_), custom_call_target="tpu_custom_call" | custom-call | tf_op jit(solution)/shard_map/stage/pallas_call | solution.py:289
  18.2 1.4 %collective-permute-start.3 = (bf16[16,32,128]{2,1,0:T(8,128)(2,1)}, bf16[16,32,128]{2,1,0:T(8,128)(2,1)S(1)}, u32[]{:S(2)}, u32[]{:S(2)}) collective-permute-start(bf16[16,32,128]{2,1,0:T(8,128)(2,1)} %get-tuple-element.37), channel_id=1, source_target_pairs={{0,4},{1,5},{2,6},{3,7},{4,0},{5,1},{6,2},{7,3},{8,12},{9,13},{10,... | collective-permute-start | bytes 393224 | tf_op jit(solution)/shard_map/ppermute | solution.py:42
  19.6 0.6 %collective-permute-start.4 = (bf16[16,32,128]{2,1,0:T(8,128)(2,1)}, bf16[16,32,128]{2,1,0:T(8,128)(2,1)S(1)}, u32[]{:S(2)}, u32[]{:S(2)}) collective-permute-start(bf16[16,32,128]{2,1,0:T(8,128)(2,1)} %get-tuple-element.37), channel_id=1, source_target_pairs={{0,2},{1,3},{2,0},{3,1},{4,6},{5,7},{6,4},{7,5},{8,10},{9,11},{10,... | collective-permute-start | bytes 393224 | tf_op jit(solution)/shard_map/ppermute | solution.py:42
  20.2 0.0 collective-permute-done.5.refs_1_
  20.2 0.0 collective-permute-done.6.refs_2_
  20.2 5.5 %stage.8 = (f32[128,896]{1,0:T(8,128)S(1)}, bf16[2,128,1024]{2,1,0:T(8,128)(2,1)S(1)}, bf16[2,128,1024]{2,1,0:T(8,128)(2,1)S(1)}) custom-call(f32[49,32,128]{2,1,0:T(8,128)S(1)} %get-tuple-element.29.refs_0_, bf16[33,32,128]{2,1,0:T(8,128)(2,1)S(1)} %collective-permute-done.5.refs_1_, bf16[33,32,128]{2,1,0:T(8,128)(2,1)S(1)} %collective-permute-done.6.refs_2_, ...), custom_call_target="tpu_custom_call" | custom-call | tf_op jit(solution)/shard_map/stage/pallas_call | solution.py:289
  25.7 1.6 %collective-permute-done.3.refs_1_ = bf16[16,32,128]{2,1,0:T(8,128)(2,1)S(1)} collective-permute-done((bf16[16,32,128]{2,1,0:T(8,128)(2,1)}, bf16[16,32,128]{2,1,0:T(8,128)(2,1)S(1)}, u32[]{:S(2)}, u32[]{:S(2)}) %collective-permute-start.3) | collective-permute-done | bytes 131104 | tf_op jit(solution)/shard_map/ppermute | solution.py:42
  27.3 0.0 collective-permute-done.4.refs_2_
  27.3 2.2 %stage.9 = bf16[128,896]{1,0:T(8,128)(2,1)S(1)} custom-call(f32[49,32,128]{2,1,0:T(8,128)S(1)} %get-tuple-element.29.refs_0_, bf16[16,32,128]{2,1,0:T(8,128)(2,1)S(1)} %collective-permute-done.3.refs_1_, bf16[16,32,128]{2,1,0:T(8,128)(2,1)S(1)} %collective-permute-done.4.refs_2_, bf16[2,128,1024]{2,1,0:T(8,128)(2,1)S(1)} %get-tuple-element.41.refs_3_, ...), custom_call_target="tpu_custom_call" | custom-call | tf_op jit(solution)/shard_map/stage/pallas_call | solution.py:289
  29.5 0.1 reshape.3
  29.5 14.3 %all_to_all.5.parts_ref = bf16[32,4,896]{2,1,0:T(4,128)(2,1)S(1)} all-to-all(bf16[32,4,896]{2,1,0:T(4,128)(2,1)S(1)} %reshape.3), channel_id=1, replica_groups=mesh['row'=4,'col'=8] {'row','col'}, dimensions={0} | all-to-all | bytes 458752 | tf_op jit(solution)/shard_map/all_to_all | solution.py:359
  43.8 0.7 %summed.1 = f32[4,896]{1,0:T(4,128)} custom-call(bf16[32,4,896]{2,1,0:T(4,128)(2,1)S(1)} %all_to_all.5.parts_ref), custom_call_target="tpu_custom_call" | custom-call | tf_op jit(solution)/shard_map/summed/pallas_call | solution.py:311
Async XLA Ops:
  2.7 5.1 %collective-permute-start = (bf16[49,32,128]{2,1,0:T(8,128)(2,1)}, bf16[49,32,128]{2,1,0:T(8,128)(2,1)S(1)}, u32[]{:S(2)}, u32[]{:S(2)}) collective-permute-start(bf16[49,32,128]{2,1,0:T(8,128)(2,1)} %get-tuple-element.26), channel_id=1, source_target_pairs={{0,1},{1,0},{2,3},{3,2},{4,5},{5,4},{6,7},{7,6},{8,9},{9,8},{10,11... | collective-permute-start | bytes 1204232 | tf_op jit(solution)/shard_map/ppermute | solution.py:42
  2.8 11.5 %collective-permute-start.1 = (bf16[33,32,128]{2,1,0:T(8,128)(2,1)}, bf16[33,32,128]{2,1,0:T(8,128)(2,1)S(1)}, u32[]{:S(2)}, u32[]{:S(2)}) collective-permute-start(bf16[33,32,128]{2,1,0:T(8,128)(2,1)} %get-tuple-element.38), channel_id=1, source_target_pairs={{0,8},{1,9},{2,10},{3,11},{4,12},{5,13},{6,14},{7,15},{8,0},{9,1},... | collective-permute-start | bytes 811016 | tf_op jit(solution)/shard_map/ppermute | solution.py:42
  5.5 14.7 %collective-permute-start.5 = (bf16[33,32,128]{2,1,0:T(8,128)(2,1)}, bf16[33,32,128]{2,1,0:T(8,128)(2,1)S(1)}, u32[]{:S(2)}, u32[]{:S(2)}) collective-permute-start(bf16[33,32,128]{2,1,0:T(8,128)(2,1)} %get-tuple-element.38), channel_id=1, source_target_pairs={{0,4},{1,5},{2,6},{3,7},{4,0},{5,1},{6,2},{7,3},{8,12},{9,13},{10,... | collective-permute-start | bytes 811016 | tf_op jit(solution)/shard_map/ppermute | solution.py:42
  7.8 12.4 %collective-permute-start.6 = (bf16[33,32,128]{2,1,0:T(8,128)(2,1)}, bf16[33,32,128]{2,1,0:T(8,128)(2,1)S(1)}, u32[]{:S(2)}, u32[]{:S(2)}) collective-permute-start(bf16[33,32,128]{2,1,0:T(8,128)(2,1)} %get-tuple-element.38), channel_id=1, source_target_pairs={{0,2},{1,3},{2,0},{3,1},{4,6},{5,7},{6,4},{7,5},{8,10},{9,11},{10,... | collective-permute-start | bytes 811016 | tf_op jit(solution)/shard_map/ppermute | solution.py:42
  9.1 7.9 %collective-permute-start.2 = (bf16[16,32,128]{2,1,0:T(8,128)(2,1)}, bf16[16,32,128]{2,1,0:T(8,128)(2,1)S(1)}, u32[]{:S(2)}, u32[]{:S(2)}) collective-permute-start(bf16[16,32,128]{2,1,0:T(8,128)(2,1)} %get-tuple-element.37), channel_id=1, source_target_pairs={{0,8},{1,9},{2,10},{3,11},{4,12},{5,13},{6,14},{7,15},{8,0},{9,1},... | collective-permute-start | bytes 393224 | tf_op jit(solution)/shard_map/ppermute | solution.py:42
  9.3 1.0 %copy-start = (bf16[49,32,128]{2,1,0:T(8,128)(2,1)S(1)}, bf16[49,32,128]{2,1,0:T(8,128)(2,1)}, u32[]{:S(2)}) copy-start(bf16[49,32,128]{2,1,0:T(8,128)(2,1)} %get-tuple-element.25.refs_0_) | copy-start | bytes 1204228
  18.2 9.1 %collective-permute-start.3 = (bf16[16,32,128]{2,1,0:T(8,128)(2,1)}, bf16[16,32,128]{2,1,0:T(8,128)(2,1)S(1)}, u32[]{:S(2)}, u32[]{:S(2)}) collective-permute-start(bf16[16,32,128]{2,1,0:T(8,128)(2,1)} %get-tuple-element.37), channel_id=1, source_target_pairs={{0,4},{1,5},{2,6},{3,7},{4,0},{5,1},{6,2},{7,3},{8,12},{9,13},{10,... | collective-permute-start | bytes 393224 | tf_op jit(solution)/shard_map/ppermute | solution.py:42
  19.6 7.7 %collective-permute-start.4 = (bf16[16,32,128]{2,1,0:T(8,128)(2,1)}, bf16[16,32,128]{2,1,0:T(8,128)(2,1)S(1)}, u32[]{:S(2)}, u32[]{:S(2)}) collective-permute-start(bf16[16,32,128]{2,1,0:T(8,128)(2,1)} %get-tuple-element.37), channel_id=1, source_target_pairs={{0,2},{1,3},{2,0},{3,1},{4,6},{5,7},{6,4},{7,5},{8,10},{9,11},{10,... | collective-permute-start | bytes 393224 | tf_op jit(solution)/shard_map/ppermute | solution.py:42
